TPU v7x, 32 devices: a whole 2x2x4 slice. The times are simulated.
32 devices in a mesh: groups: 2 (over y), sect: 16 (over z, x, core).
Axes of the slice: x: 2, y: 2, z: 4, core: 2. Of those that a mesh axis runs over, the one named last changes fastest.
Arguments:
- wavefunction: bfloat16 [512, 8, 128, 128], P(('groups', 'sect')), parts along dimension 0, may hold values from -6 to 6
- left_environment: bfloat16 [512, 2, 128, 128], P(('groups', 'sect')), parts along dimension 0, may hold values from -0.5 to 0.5
- right_environment: bfloat16 [128, 2, 128, 128], P(('groups', 'sect')), parts along dimension 0, may hold values from -0.5 to 0.5
- left_length: int32 [512], P(('groups', 'sect')), parts along dimension 0, may hold values from 64 to 128
- right_length: int32 [128], P(('groups', 'sect')), parts along dimension 0, may hold values from 64 to 128
- right_owner: int32 [512, 8], P(('groups', 'sect')), parts along dimension 0, may hold values from 0 to 15, all different within a row; in each aligned block of 16 rows (0 to 15, 16 to 31, ...) at most 8 rows name the same one
- right_slot: int32 [512, 8], P(('groups', 'sect')), parts along dimension 0, may hold values from 0 to 3
Outputs:
- hpsi: bfloat16 [512, 8, 128, 128], P(('groups', 'sect')), parts along dimension 0
There are 2 independent parts, one for each index of `groups`. A program takes and returns all parts, laid end to end along the dimension named above; each array names one. Nothing has to cross between parts.
Inputs may be any that keep to these rules, and one draw needn't show every extreme that they name: `right_owner`: the 8 owners of one left sector are distinct; the 16 left sectors of one device name one owner at most 8 times in all, a bound that some block reaches by some device's left sectors.
All inputs are finite; a program needn't handle non-finite values.
Results may differ from a plain program's by a relative error of at most 0.0049.
Values may be sent and summed in bfloat16 or wider, within the bound.
No kernel may reach another device: no remote copies, remote signals or barrier semaphores. Data moves between devices by JAX's collectives and lax.ppermute only.
A program may use at most 128 MiB of HBM per device.

v0:
```python
import jax
import jax.numpy as jnp
from jax import lax
from jax.sharding import PartitionSpec as P


def mask_blocks(blocks, lengths):
    indices = jnp.arange(blocks.shape[-1], dtype=jnp.int32)
    live_rows = indices[None, :] < lengths[:, None]
    keep = live_rows[:, :, None] & live_rows[:, None, :]
    return jnp.where(keep[:, None, :, :], blocks, jnp.zeros_like(blocks))


def local(
    wavefunction,
    left_environment,
    right_environment,
    left_length,
    right_length,
    right_owner,
    right_slot,
):
    sector_count = wavefunction.shape[0]
    partner_count = wavefunction.shape[1]
    block_size = wavefunction.shape[-1]
    term_count = left_environment.shape[1]
    local_right = right_environment.shape[0]
    left_live = mask_blocks(left_environment, left_length)
    right_live = mask_blocks(right_environment, right_length)
    partial_value = jnp.einsum(
        "akpq,ajqr->ajkpr", left_live, wavefunction, preferred_element_type=jnp.float32
    ).astype(jnp.bfloat16)
    block_count = sector_count * partner_count
    owners = right_owner.reshape(block_count)
    slots = right_slot.reshape(block_count)
    everyone = lax.all_gather(right_live, "sect", axis=0, tiled=True)
    destination = owners * local_right + slots
    chosen = jnp.take(everyone, destination, axis=0).reshape(
        sector_count, partner_count, term_count, block_size, block_size
    )
    hpsi = jnp.einsum(
        "ajkpr,ajkcr->ajpc", partial_value, chosen, preferred_element_type=jnp.float32
    ).astype(jnp.bfloat16)
    return hpsi


def solution(mesh):
    return jax.shard_map(
        local,
        mesh=mesh,
        in_specs=(
            P(("groups", "sect"), None, None, None),
            P(("groups", "sect"), None, None, None),
            P(("groups", "sect"), None, None, None),
            P(("groups", "sect")),
            P(("groups", "sect")),
            P(("groups", "sect"), None),
            P(("groups", "sect"), None),
        ),
        out_specs=P(("groups", "sect"), None, None, None),
        check_vma=False,
    )
```

profile of v0, /device:TPU:0, one launch (start us, length us, event | category | flops | bytes accessed | tf_op | source)
XLA Modules:
  0.0 87.2 jit_solution(6862495238078279326)
XLA Ops:
  6.5 0.0 all-gather.2.cloned.1.call-start
  6.5 0.7 iota_compare_fusion.1
  7.3 0.1 broadcast_and_fusion.1
  7.4 1.7 %broadcast_select_fusion = bf16[4,2,128,128]{3,2,1,0:T(8,128)(2,1)} fusion(bf16[4,2,128,128]{3,2,1,0:T(8,128)(2,1)} %param.9, pred[4,128,128]{2,1,0:T(8,128)(4,1)S(1)} %broadcast_and_fusion.1), kind=kLoop, calls=%fused_computation.15 | loop fusion | flops 131072 | bytes 589824 | tf_op jit(solution)/shard_map/jit(_where)/select_n | solution.py:11
  9.1 0.0 all-gather.2.cloned.1.call-update
  9.1 0.7 compare_and_fusion
  9.8 0.1 copy.13
  9.9 0.1 add.41
  10.0 0.1 copy.12
  10.1 0.7 iota_compare_fusion
  10.8 0.3 broadcast_and_fusion
  11.2 0.0 copy-start
  11.2 51.6 %all-gather.2.cloned.1.call-done = bf16[64,2,128,128]{3,2,1,0:T(8,128)(2,1)} async-done(((bf16[4,2,128,128]{3,2,1,0:T(8,128)(2,1)}), bf16[64,2,128,128]{3,2,1,0:T(8,128)(2,1)}) %all-gather.2.cloned.1.call-update) | async-done | bytes 4194320 | tf_op jit(solution)/shard_map/all_gather | solution.py:36
  62.8 8.7 %gather_fusion = bf16[128,2,128,128]{3,2,1,0:T(8,128)(2,1)} fusion(bf16[64,2,128,128]{3,2,1,0:T(8,128)(2,1)} %all-gather.2.cloned.1.call-done, s32[1024]{0:T(1024)S(1)} %pad_clamp_fusion), kind=kCustom, calls=%fused_computation | custom fusion | bytes 16777728 | tf_op jit(solution)/shard_map/jit(_take)/gather | solution.py:38
  71.5 0.0 copy-done
  71.5 8.8 %bitcast_convert_fusion = bf16[16,8,128,128]{3,2,1,0:T(8,128)(2,1)} fusion(bf16[16,8,2,128,128]{4,3,2,1,0:T(8,128)(2,1)} %bitcast.25, pred[16,8]{1,0:T(8,128)(4,1)S(1)} %copy.12, bf16[16,8,128,128]{3,2,1,0:T(8,128)(2,1)} %param.7, bf16[16,2,128,128]{3,2,1,0:T(8,128)(2,1)S(1)} %copy-done, pred[16,128,128]{2,1,0:T(8,128)(4,1)S(1)} %broadcast_and_fusion), kind=kOutput, calls=%fused_computation.1 | convolution fusion | flops 2158493696 | bytes 18088064 | tf_op jit(solution)/shard_map/ajkpr,ajkcr->ajpc/dot_general | solution.py:41
  (2 shorter events, 0.0 us)
Async XLA Ops:
  6.5 56.3 %all-gather.2.cloned.1.call-start = ((), (), s32[]{:S(2)}) async-start(), calls=%async_computation | async-start | bytes 4456448 | tf_op jit(solution)/shard_map/all_gather | solution.py:36
  11.2 60.4 %copy-start = (bf16[16,2,128,128]{3,2,1,0:T(8,128)(2,1)S(1)}, bf16[16,2,128,128]{3,2,1,0:T(8,128)(2,1)}, u32[]{:S(2)}) copy-start(bf16[16,2,128,128]{3,2,1,0:T(8,128)(2,1)} %param.8) | copy-start | bytes 3145732
Sparse Core Ops, SparseCore 0:
  9.5 53.2 all-gather.1
where the time goes:
time: 87.5 us; the launch traced here: 87.2 us
  waiting for transfers between devices  51.6 us (59%)
  between operations  13.4 us (15%)
  local copies, waits for them, and re-layouts  8.98 us (10%)
  matrix products  8.84 us (10%)
  other arithmetic  4.34 us (5%)
    all_gather x1, waiting for transfers between devices, local(): everyone = lax.all_gather(right_live, 'sect', axis=0, tiled=True)  51.6 us
    dot_general x1, matrix products, local(): jnp.einsum('ajkpr,ajkcr->ajpc', partial_value, chosen, preferred_element_...  8.84 us
    gather x1, local copies, waits for them, and re-layouts, local(): jnp.take(everyone, destination, axis=0)  8.73 us
  transfers between devices with their start and end apart: 1, of which 1 were waited for; matrix products, arithmetic and copies ran while one was open for 2% of the time, Pallas kernels for 0%

commit v1 on v0

v1 whole, which is shorter than its diff:
```python
import functools

import jax
import jax.numpy as jnp
import numpy as np
from jax import lax
from jax.experimental import pallas as pl
from jax.experimental.pallas import tpu as pltpu
from jax.sharding import PartitionSpec as P

SMEM = pl.BlockSpec(memory_space=pltpu.SMEM)
VMEM = pl.BlockSpec(memory_space=pltpu.VMEM)
ANY = pl.BlockSpec(memory_space=pl.ANY)


def live(size, length):
    rows = lax.broadcasted_iota(jnp.int32, (size, size), 0)
    columns = lax.broadcasted_iota(jnp.int32, (size, size), 1)
    return (rows < length) & (columns < length)


def mask_kernel(length_ref, blocks_ref, out_ref):
    sectors, terms, size, _ = blocks_ref.shape
    for b in range(sectors):
        keep = live(size, length_ref[b])
        for k in range(terms):
            block = blocks_ref[b, k]
            out_ref[b, k] = jnp.where(keep, block, jnp.zeros_like(block))


def mask_right(lengths, blocks):
    return pl.pallas_call(
        mask_kernel,
        in_specs=[SMEM, VMEM],
        out_specs=VMEM,
        out_shape=pltpu.VMEM(blocks.shape, blocks.dtype),
        name="mask_right",
    )(lengths, blocks)


def partial_kernel(cap, slots, length_ref, place_ref, owner_ref, slot_ref, left_ref, wave_ref, partial_ref, work_ref, count_ref):
    step = pl.program_id(0)
    sectors, partners, size, _ = wave_ref.shape

    @pl.when(step == 0)
    def _():
        for c in range(count_ref.shape[0]):
            count_ref[c] = 0

    for s in range(sectors):
        a = step * sectors + s
        keep = live(size, length_ref[a])
        left = left_ref[s]
        left = jnp.where(keep[None], left, jnp.zeros_like(left))
        for j in range(partners):
            wave = wave_ref[s, j]
            for k in range(left.shape[0]):
                term = jnp.dot(left[k], wave, preferred_element_type=jnp.float32)
                partial_ref[a * partners + j, :, k * size:(k + 1) * size] = term.astype(partial_ref.dtype)
        for j in range(partners):
            chunk = place_ref[owner_ref[j, a]]
            filled = count_ref[chunk]
            count_ref[chunk] = filled + 1
            work_ref[chunk * cap + filled] = (a * partners + j) * slots + slot_ref[j, a]


def partials(cap, slots, lengths, place, owner, slot, left, wave):
    sectors, partners, size, _ = wave.shape
    terms, n = left.shape[1], place.shape[0]
    step = 2
    return pl.pallas_call(
        functools.partial(partial_kernel, cap, slots),
        grid=(sectors // step,),
        in_specs=[
            SMEM, SMEM, SMEM, SMEM,
            pl.BlockSpec((step, terms, size, size), lambda i: (i, 0, 0, 0)),
            pl.BlockSpec((step, partners, size, size), lambda i: (i, 0, 0, 0)),
        ],
        out_specs=[VMEM, SMEM, SMEM],
        out_shape=[
            pltpu.VMEM((sectors * partners, size, terms * size), wave.dtype),
            jax.ShapeDtypeStruct((n * cap,), jnp.int32),
            jax.ShapeDtypeStruct((n,), jnp.int32),
        ],
        compiler_params=pltpu.CompilerParams(vmem_limit_bytes=16 << 20),
        cost_estimate=pl.CostEstimate(
            flops=2 * sectors * partners * terms * size**3,
            bytes_accessed=2 * wave.size + 2 * left.size, transcendentals=0,
        ),
        name="partials",
    )(lengths, place, owner, slot, left, wave)


def product_kernel(first, cap, exact, slots, chunks, aliased, work_ref, count_ref, partial_ref, *refs):
    right_refs, out_ref, stage, sem = refs[:chunks], refs[chunks + aliased], refs[-2], refs[-1]
    partners = out_ref.shape[1]
    terms = right_refs[0].shape[1]

    def copy(at, index):
        return pltpu.make_async_copy(
            stage.at[at], out_ref.at[lax.div(index, partners), lax.rem(index, partners)], sem)

    for c in range(chunks):
        for i in range(cap):
            def item(c=c, i=i):
                entry = work_ref[(first + c) * cap + i]
                index, slot = lax.div(entry, slots), lax.rem(entry, slots)
                right = jnp.concatenate([right_refs[c][slot, k] for k in range(terms)], axis=1)
                stage[c * cap + i] = lax.dot_general(
                    partial_ref[index], right, (((1,), (1,)), ((), ())), preferred_element_type=jnp.float32,
                ).astype(stage.dtype)
                copy(c * cap + i, index).start()
            if exact:
                item()
            else:
                pl.when(i < count_ref[first + c])(item)
    if exact:
        whole = out_ref.at[pl.ds(0, chunks * cap // partners)]
        pltpu.make_async_copy(whole, whole, sem).wait()
    else:
        for c in range(chunks):
            for i in range(cap):
                @pl.when(i < count_ref[first + c])
                def _(c=c, i=i):
                    copy(c * cap + i, 0).wait()


def products(first, cap, exact, out_shape, work, count, partial_value, rights, out):
    chunks, aliased = len(rights), out is not None
    size = out_shape.shape[-1]
    rights = [pltpu.with_memory_space_constraint(r, pltpu.VMEM) for r in rights]
    partial_value = pltpu.with_memory_space_constraint(partial_value, pltpu.VMEM)
    return pl.pallas_call(
        functools.partial(product_kernel, first, cap, exact, rights[0].shape[0], chunks, aliased),
        in_specs=[SMEM, SMEM, VMEM] + [VMEM] * chunks + [ANY] * aliased,
        out_specs=ANY,
        out_shape=out_shape,
        scratch_shapes=[
            pltpu.VMEM((chunks * cap, size, size), out_shape.dtype),
            pltpu.SemaphoreType.DMA,
        ],
        input_output_aliases={3 + chunks: 0} if aliased else {},
        compiler_params=pltpu.CompilerParams(vmem_limit_bytes=16 << 20),
        cost_estimate=pl.CostEstimate(
            flops=2 * chunks * cap * 2 * size**3,
            bytes_accessed=2 * chunks * cap * size**2, transcendentals=0,
        ),
        name="products",
    )(work, count, partial_value, *rights, *([out] if aliased else []))


def local(n, wavefunction, left_environment, right_environment, left_length, right_length, right_owner, right_slot):
    sectors, partners = wavefunction.shape[:2]
    blocks = sectors * partners
    slots = right_environment.shape[0]
    cap = max(2, blocks // n)
    exact = cap * n == blocks
    chips = n // 2
    ring = list(range(0, chips, 2)) + list(range(chips - 1, 0, -2))
    at = {chip: i for i, chip in enumerate(ring)}
    onward = [(ring[i] * 2, ring[(i + 1) % chips] * 2) for i in range(chips)]
    onward += [(ring[i] * 2 + 1, ring[(i - 1) % chips] * 2 + 1) for i in range(chips)]
    across = [(d, d ^ 1) for d in range(n)]

    def origin(device, hop, other, via):
        chip, core = device // 2, device % 2
        carrier = core ^ via
        step = hop if carrier == 0 else -hop
        return ring[(at[chip] - step) % chips] * 2 + (carrier ^ other)

    plan = [(0, 0, 0), (0, 1, 0)]
    for hop in range(1, chips // 2 + 1):
        for other in (0, 1) if hop < chips // 2 else (0,):
            plan += [(hop, other, 0), (hop, other, 1)]
    place = np.zeros((n, n), np.int32)
    for device in range(n):
        for c, (hop, other, via) in enumerate(plan):
            place[device, origin(device, hop, other, via)] = c
    assert len(plan) == n

    me = lax.axis_index("sect")
    mine = mask_right(right_length, right_environment)
    send = functools.partial(lax.ppermute, axis_name="sect")
    chunks = [mine, send(mine, perm=across)]
    here = list(chunks)
    for hop in range(1, chips // 2 + 1):
        for other in (0, 1) if hop < chips // 2 else (0,):
            here[other] = send(here[other], perm=onward)
            chunks += [here[other], send(here[other], perm=across)]
    partial_value, work, count = partials(
        cap, slots, left_length, jnp.asarray(place)[me], right_owner.T, right_slot.T, left_environment, wavefunction)
    out_shape = jax.ShapeDtypeStruct(wavefunction.shape, wavefunction.dtype)
    out = None
    cuts = [0, 6, 10, 14, 16] if n == 16 else list(range(0, n, 16)) + [n]
    for low, high in zip(cuts, cuts[1:]):
        out = products(low, cap, exact, out_shape, work, count, partial_value, chunks[low:high], out)
    return out


def solution(mesh):
    split = ("groups", "sect")
    return jax.shard_map(
        functools.partial(local, mesh.shape["sect"]),
        mesh=mesh,
        in_specs=(
            P(split, None, None, None),
            P(split, None, None, None),
            P(split, None, None, None),
            P(split),
            P(split),
            P(split, None),
            P(split, None),
        ),
        out_specs=P(split, None, None, None),
        check_vma=False,
    )
```

time: 87.5 us -> 46.8 us (0.53)
  waiting for transfers between devices: 51.6 us -> 9.86 us
  starting transfers between devices: 0.01 us -> 16.7 us
  Pallas kernels: 0 us -> 13.7 us
  between operations: 13.4 us -> 0.1 us
  matrix products: 8.84 us -> 0 us
  other arithmetic: 4.34 us -> 0 us
  local copies, waits for them, and re-layouts: 8.98 us -> 6.13 us
    all_gather x1 -> x0, waiting for transfers between devices: 51.6 us -> none  [local(): everyone = lax.all_gather(right_live, 'sect', axis=0, tiled=True)]
    ppermute x0 -> x15, starting transfers between devices: none -> 16.7 us  [the longest x7 14.7 us: local(): here[other] = send(here[other], perm=onward)]
    pallas_call x0 -> x6, Pallas kernels: none -> 13.7 us  [the longest x4 7.71 us: products(): pl.pallas_call(functools.partial(product_kernel, first, cap, exact, right...]
    ppermute x0 -> x15, waiting for transfers between devices: none -> 9.86 us  [the longest x7 9.84 us: local(): here[other] = send(here[other], perm=onward)]
    dot_general x1 -> x0, matrix products: 8.84 us -> none  [local(): jnp.einsum('ajkpr,ajkcr->ajpc', partial_value, chosen, preferred_element_...]
    gather x1 -> x0, local copies, waits for them, and re-layouts: 8.73 us -> none  [local(): jnp.take(everyone, destination, axis=0)]
    unnamed x2 -> x10, local copies, waits for them, and re-layouts: 0.01 us -> 5.44 us
    select_n x2 -> x0, other arithmetic: 1.68 us -> none  [the longest x1 1.68 us: mask_blocks(): return jnp.where(keep[:, None, :, :], blocks, jnp.zeros_like(blocks))]
  transfers between devices with their start and end apart: 1 -> 15, of which waited for: 1 -> 7; matrix products, arithmetic and copies ran while one was open for 2% -> 1% of each run, Pallas kernels for 0% -> 24%
where the time goes in v1:
time: 46.8 us; the launch traced here: 46.5 us
  starting transfers between devices  16.7 us (36%)
  Pallas kernels  13.7 us (29%)
  waiting for transfers between devices  9.86 us (21%)
  local copies, waits for them, and re-layouts  6.13 us (13%)
    ppermute x7, starting transfers between devices, local(): here[other] = send(here[other], perm=onward)  14.7 us
    ppermute x7, waiting for transfers between devices, local(): here[other] = send(here[other], perm=onward)  9.84 us
    pallas_call x4, Pallas kernels, products(): pl.pallas_call(functools.partial(product_kernel, first, cap, exact, right...  7.71 us
    unnamed x10, local copies, waits for them, and re-layouts  5.44 us
    pallas_call x1, Pallas kernels, partials(): pl.pallas_call(functools.partial(partial_kernel, cap, slots), grid=(secto...  4.99 us
    ppermute x7, starting transfers between devices, local(): chunks += [here[other], send(here[other], perm=across)]  1.42 us
    pallas_call x1, Pallas kernels, mask_right(): pl.pallas_call(mask_kernel, in_specs=[SMEM, VMEM], out_specs=VMEM, out_sh...  1.03 us
  transfers between devices with their start and end apart: 15, of which 7 were waited for; matrix products, arithmetic and copies ran while one was open for 1% of the time, Pallas kernels for 24%

profile of v1, /device:TPU:0, one launch (start us, length us, event | category | flops | bytes accessed | tf_op | source)
XLA Modules:
  0.0 46.5 jit_solution(10442571744469722134)
XLA Ops:
  0.0 1.0 %mask_right.1.refs_0_ = bf16[4,2,128,128]{3,2,1,0:T(8,128)(2,1)S(1)} custom-call(s32[4]{0:T(128)} %length_ref.3, bf16[4,2,128,128]{3,2,1,0:T(8,128)(2,1)} %blocks_ref.1), custom_call_target="tpu_custom_call" | custom-call | tf_op jit(solution)/shard_map/mask_right/pallas_call | solution.py:32
  1.6 2.6 %collective-permute-start = (bf16[4,2,128,128]{3,2,1,0:T(8,128)(2,1)S(1)}, bf16[4,2,128,128]{3,2,1,0:T(8,128)(2,1)S(1)}, u32[]{:S(2)}, u32[]{:S(2)}) collective-permute-start(bf16[4,2,128,128]{3,2,1,0:T(8,128)(2,1)S(1)} %mask_right.1.refs_0_), channel_id=1, source_target_pairs={{0,4},{4,8},{8,12},{12,14},{14,10},{10,6},{6,2},{2,0},{1,3},{5,1},... | collective-permute-start | bytes 786440 | tf_op jit(solution)/shard_map/ppermute | solution.py:188
  4.2 1.6 %collective-permute-start.7 = (bf16[4,2,128,128]{3,2,1,0:T(8,128)(2,1)S(1)}, bf16[4,2,128,128]{3,2,1,0:T(8,128)(2,1)S(1)}, u32[]{:S(2)}, u32[]{:S(2)}) collective-permute-start(bf16[4,2,128,128]{3,2,1,0:T(8,128)(2,1)S(1)} %collective-permute-done.6.refs_1_), channel_id=1, source_target_pairs={{0,4},{4,8},{8,12},{12,14},{14,10},{10,6},{6,2},{2,0},{1,3},{5,1},... | collective-permute-start | bytes 786440 | tf_op jit(solution)/shard_map/ppermute | solution.py:188
  5.8 2.7 %collective-permute-done.refs_2_ = bf16[4,2,128,128]{3,2,1,0:T(8,128)(2,1)S(1)} collective-permute-done((bf16[4,2,128,128]{3,2,1,0:T(8,128)(2,1)S(1)}, bf16[4,2,128,128]{3,2,1,0:T(8,128)(2,1)S(1)}, u32[]{:S(2)}, u32[]{:S(2)}) %collective-permute-start) | collective-permute-done | bytes 262176 | tf_op jit(solution)/shard_map/ppermute | solution.py:188
  8.5 2.1 %collective-permute-start.1 = (bf16[4,2,128,128]{3,2,1,0:T(8,128)(2,1)S(1)}, bf16[4,2,128,128]{3,2,1,0:T(8,128)(2,1)S(1)}, u32[]{:S(2)}, u32[]{:S(2)}) collective-permute-start(bf16[4,2,128,128]{3,2,1,0:T(8,128)(2,1)S(1)} %collective-permute-done.refs_2_), channel_id=1, source_target_pairs={{0,4},{4,8},{8,12},{12,14},{14,10},{10,6},{6,2},{2,0},{1,3},{5,1},... | collective-permute-start | bytes 786440 | tf_op jit(solution)/shard_map/ppermute | solution.py:188
  10.6 0.7 %collective-permute-done.7.refs_4_ = bf16[4,2,128,128]{3,2,1,0:T(8,128)(2,1)S(1)} collective-permute-done((bf16[4,2,128,128]{3,2,1,0:T(8,128)(2,1)S(1)}, bf16[4,2,128,128]{3,2,1,0:T(8,128)(2,1)S(1)}, u32[]{:S(2)}, u32[]{:S(2)}) %collective-permute-start.7) | collective-permute-done | bytes 262176 | tf_op jit(solution)/shard_map/ppermute | solution.py:188
  11.3 2.1 %collective-permute-start.8 = (bf16[4,2,128,128]{3,2,1,0:T(8,128)(2,1)S(1)}, bf16[4,2,128,128]{3,2,1,0:T(8,128)(2,1)S(1)}, u32[]{:S(2)}, u32[]{:S(2)}) collective-permute-start(bf16[4,2,128,128]{3,2,1,0:T(8,128)(2,1)S(1)} %collective-permute-done.7.refs_4_), channel_id=1, source_target_pairs={{0,4},{4,8},{8,12},{12,14},{14,10},{10,6},{6,2},{2,0},{1,3},{5,1},... | collective-permute-start | bytes 786440 | tf_op jit(solution)/shard_map/ppermute | solution.py:188
  13.4 1.5 %collective-permute-done.1.refs_0_ = bf16[4,2,128,128]{3,2,1,0:T(8,128)(2,1)S(1)} collective-permute-done((bf16[4,2,128,128]{3,2,1,0:T(8,128)(2,1)S(1)}, bf16[4,2,128,128]{3,2,1,0:T(8,128)(2,1)S(1)}, u32[]{:S(2)}, u32[]{:S(2)}) %collective-permute-start.1) | collective-permute-done | bytes 262176 | tf_op jit(solution)/shard_map/ppermute | solution.py:188
  14.8 2.1 %collective-permute-start.2 = (bf16[4,2,128,128]{3,2,1,0:T(8,128)(2,1)S(1)}, bf16[4,2,128,128]{3,2,1,0:T(8,128)(2,1)S(1)}, u32[]{:S(2)}, u32[]{:S(2)}) collective-permute-start(bf16[4,2,128,128]{3,2,1,0:T(8,128)(2,1)S(1)} %collective-permute-done.1.refs_0_), channel_id=1, source_target_pairs={{0,4},{4,8},{8,12},{12,14},{14,10},{10,6},{6,2},{2,0},{1,3},{5,1},... | collective-permute-start | bytes 786440 | tf_op jit(solution)/shard_map/ppermute | solution.py:188
  17.6 2.1 %collective-permute-start.9 = (bf16[4,2,128,128]{3,2,1,0:T(8,128)(2,1)S(1)}, bf16[4,2,128,128]{3,2,1,0:T(8,128)(2,1)S(1)}, u32[]{:S(2)}, u32[]{:S(2)}) collective-permute-start(bf16[4,2,128,128]{3,2,1,0:T(8,128)(2,1)S(1)} %collective-permute-done.8.refs_2_), channel_id=1, source_target_pairs={{0,4},{4,8},{8,12},{12,14},{14,10},{10,6},{6,2},{2,0},{1,3},{5,1},... | collective-permute-start | bytes 786440 | tf_op jit(solution)/shard_map/ppermute | solution.py:188
  19.8 1.5 %collective-permute-done.2.refs_0_ = bf16[4,2,128,128]{3,2,1,0:T(8,128)(2,1)S(1)} collective-permute-done((bf16[4,2,128,128]{3,2,1,0:T(8,128)(2,1)S(1)}, bf16[4,2,128,128]{3,2,1,0:T(8,128)(2,1)S(1)}, u32[]{:S(2)}, u32[]{:S(2)}) %collective-permute-start.2) | collective-permute-done | bytes 262176 | tf_op jit(solution)/shard_map/ppermute | solution.py:188
  21.2 2.1 %collective-permute-start.3 = (bf16[4,2,128,128]{3,2,1,0:T(8,128)(2,1)S(1)}, bf16[4,2,128,128]{3,2,1,0:T(8,128)(2,1)S(1)}, u32[]{:S(2)}, u32[]{:S(2)}) collective-permute-start(bf16[4,2,128,128]{3,2,1,0:T(8,128)(2,1)S(1)} %collective-permute-done.2.refs_0_), channel_id=1, source_target_pairs={{0,4},{4,8},{8,12},{12,14},{14,10},{10,6},{6,2},{2,0},{1,3},{5,1},... | collective-permute-start | bytes 786440 | tf_op jit(solution)/shard_map/ppermute | solution.py:188
  24.3 3.2 %collective-permute-done.3.refs_0_ = bf16[4,2,128,128]{3,2,1,0:T(8,128)(2,1)S(1)} collective-permute-done((bf16[4,2,128,128]{3,2,1,0:T(8,128)(2,1)S(1)}, bf16[4,2,128,128]{3,2,1,0:T(8,128)(2,1)S(1)}, u32[]{:S(2)}, u32[]{:S(2)}) %collective-permute-start.3) | collective-permute-done | bytes 262176 | tf_op jit(solution)/shard_map/ppermute | solution.py:188
  27.6 0.7 %dynamic-slice_bitcast_fusion.place_ref = s32[16]{0:T(128)S(1)} fusion(s32[16,16]{1,0:T(8,128)} %constant.10.clone, s32[]{:T(128)S(6)} %select_n.3), kind=kLoop, calls=%fused_computation | loop fusion | bytes 132 | tf_op jit(solution)/shard_map/squeeze | solution.py:191
  28.3 2.2 %copy-done = bf16[16,8,128,128]{3,2,1,0:T(8,128)(2,1)S(1)} copy-done((bf16[16,8,128,128]{3,2,1,0:T(8,128)(2,1)S(1)}, bf16[16,8,128,128]{3,2,1,0:T(8,128)(2,1)}, u32[]{:S(2)}) %copy-start) | copy-done | bytes 4194328
  30.5 1.2 %copy-done.1 = bf16[16,2,128,128]{3,2,1,0:T(8,128)(2,1)S(1)} copy-done((bf16[16,2,128,128]{3,2,1,0:T(8,128)(2,1)S(1)}, bf16[16,2,128,128]{3,2,1,0:T(8,128)(2,1)}, u32[]{:S(2)}) %copy-start.1) | copy-done | bytes 1048600
  31.7 0.7 %copy-done.2 = s32[16,8]{0,1:T(8,128)S(1)} copy-done((s32[16,8]{0,1:T(8,128)S(1)}, s32[16,8]{0,1:T(8,128)}, u32[]{:S(2)}) %copy-start.2) | copy-done | bytes 536
  32.4 0.7 %copy-done.3 = s32[16,8]{0,1:T(8,128)S(1)} copy-done((s32[16,8]{0,1:T(8,128)S(1)}, s32[16,8]{0,1:T(8,128)}, u32[]{:S(2)}) %copy-start.3) | copy-done | bytes 536
  33.1 0.7 %copy-done.4 = s32[16]{0:T(128)S(1)} copy-done((s32[16]{0:T(128)S(1)}, s32[16]{0:T(128)}, u32[]{:S(2)}) %copy-start.4) | copy-done | bytes 88
  33.7 5.0 %partials.1 = (bf16[128,128,256]{2,1,0:T(8,128)(2,1)S(1)}, s32[128]{0:T(128)S(1)}, s32[16]{0:T(128)S(1)}) custom-call(s32[16]{0:T(128)S(1)} %copy-done.4, s32[16]{0:T(128)S(1)} %dynamic-slice_bitcast_fusion.place_ref, s32[8,16]{1,0:T(8,128)S(1)} %bitcast.4, s32[8,16]{1,0:T(8,128)S(1)} %bitcast.5, bf16[16,2,128,128]{3,2,1,0:T(8,128)(2,1)S(1)} %copy-done.1, ...), custom_call_target="tpu_custom_call" | custom-call | flops 1073741824 | bytes 5242880 | tf_op jit(solution)/shard_map/partials/pallas_call | solution.py:71
  38.7 2.2 %products.4.refs_4_ = bf16[16,8,128,128]{3,2,1,0:T(8,128)(2,1)} custom-call(s32[128]{0:T(128)S(1)} %get-tuple-element.8.work_ref, s32[16]{0:T(128)S(1)} %get-tuple-element.9.count_ref, bf16[128,128,256]{2,1,0:T(8,128)(2,1)S(1)} %get-tuple-element.10.partial_ref, bf16[4,2,128,128]{3,2,1,0:T(8,128)(2,1)S(1)} %mask_right.1.refs_0_, ...), custom_call_target="tpu_custom_call" | custom-call | flops 402653184 | bytes 1572864 | tf_op jit(solution)/shard_map/products/pallas_call | solution.py:133
  41.0 1.9 %products.5.refs_4_ = bf16[16,8,128,128]{3,2,1,0:T(8,128)(2,1)} custom-call(s32[128]{0:T(128)S(1)} %get-tuple-element.8.work_ref, s32[16]{0:T(128)S(1)} %get-tuple-element.9.count_ref, bf16[128,128,256]{2,1,0:T(8,128)(2,1)S(1)} %get-tuple-element.10.partial_ref, ...), custom_call_target="tpu_custom_call", output_to_operand_aliasing={{}: (7, {})} | custom-call | flops 268435456 | bytes 1048576 | tf_op jit(solution)/shard_map/products/pallas_call | solution.py:133
  42.9 1.9 %products.6.refs_2_ = bf16[16,8,128,128]{3,2,1,0:T(8,128)(2,1)} custom-call(s32[128]{0:T(128)S(1)} %get-tuple-element.8.work_ref, s32[16]{0:T(128)S(1)} %get-tuple-element.9.count_ref, bf16[128,128,256]{2,1,0:T(8,128)(2,1)S(1)} %get-tuple-element.10.partial_ref, ...), custom_call_target="tpu_custom_call", output_to_operand_aliasing={{}: (7, {})} | custom-call | flops 268435456 | bytes 1048576 | tf_op jit(solution)/shard_map/products/pallas_call | solution.py:133
  44.9 1.6 %products.7 = bf16[16,8,128,128]{3,2,1,0:T(8,128)(2,1)} custom-call(s32[128]{0:T(128)S(1)} %get-tuple-element.8.work_ref, s32[16]{0:T(128)S(1)} %get-tuple-element.9.count_ref, bf16[128,128,256]{2,1,0:T(8,128)(2,1)S(1)} %get-tuple-element.10.partial_ref, bf16[4,2,128,128]{3,2,1,0:T(8,128)(2,1)S(1)} %collective-permute-done.3.refs_0_, ...), custom_call_target="tpu_custom_call", output_to_operand_aliasing={{}: (5, {})} | custom-call | flops 134217728 | bytes 524288 | tf_op jit(solution)/shard_map/products/pallas_call | solution.py:133
  (23 shorter events, 2.3 us)
Async XLA Ops:
  1.0 3.2 %collective-permute-start.6 = (bf16[4,2,128,128]{3,2,1,0:T(8,128)(2,1)S(1)}, bf16[4,2,128,128]{3,2,1,0:T(8,128)(2,1)S(1)}, u32[]{:S(2)}, u32[]{:S(2)}) collective-permute-start(bf16[4,2,128,128]{3,2,1,0:T(8,128)(2,1)S(1)} %mask_right.1.refs_0_), channel_id=1, source_target_pairs={{0,1},{1,0},{2,3},{3,2},{4,5},{5,4},{6,7},{7,6},{8,9},{9,8},{10,11... | collective-permute-start | bytes 786440 | tf_op jit(solution)/shard_map/ppermute | solution.py:184
  1.6 6.9 %collective-permute-start = (bf16[4,2,128,128]{3,2,1,0:T(8,128)(2,1)S(1)}, bf16[4,2,128,128]{3,2,1,0:T(8,128)(2,1)S(1)}, u32[]{:S(2)}, u32[]{:S(2)}) collective-permute-start(bf16[4,2,128,128]{3,2,1,0:T(8,128)(2,1)S(1)} %mask_right.1.refs_0_), channel_id=1, source_target_pairs={{0,4},{4,8},{8,12},{12,14},{14,10},{10,6},{6,2},{2,0},{1,3},{5,1},... | collective-permute-start | bytes 786440 | tf_op jit(solution)/shard_map/ppermute | solution.py:188
  4.2 7.1 %collective-permute-start.7 = (bf16[4,2,128,128]{3,2,1,0:T(8,128)(2,1)S(1)}, bf16[4,2,128,128]{3,2,1,0:T(8,128)(2,1)S(1)}, u32[]{:S(2)}, u32[]{:S(2)}) collective-permute-start(bf16[4,2,128,128]{3,2,1,0:T(8,128)(2,1)S(1)} %collective-permute-done.6.refs_1_), channel_id=1, source_target_pairs={{0,4},{4,8},{8,12},{12,14},{14,10},{10,6},{6,2},{2,0},{1,3},{5,1},... | collective-permute-start | bytes 786440 | tf_op jit(solution)/shard_map/ppermute | solution.py:188
  8.5 6.4 %collective-permute-start.1 = (bf16[4,2,128,128]{3,2,1,0:T(8,128)(2,1)S(1)}, bf16[4,2,128,128]{3,2,1,0:T(8,128)(2,1)S(1)}, u32[]{:S(2)}, u32[]{:S(2)}) collective-permute-start(bf16[4,2,128,128]{3,2,1,0:T(8,128)(2,1)S(1)} %collective-permute-done.refs_2_), channel_id=1, source_target_pairs={{0,4},{4,8},{8,12},{12,14},{14,10},{10,6},{6,2},{2,0},{1,3},{5,1},... | collective-permute-start | bytes 786440 | tf_op jit(solution)/shard_map/ppermute | solution.py:188
  11.3 6.4 %collective-permute-start.8 = (bf16[4,2,128,128]{3,2,1,0:T(8,128)(2,1)S(1)}, bf16[4,2,128,128]{3,2,1,0:T(8,128)(2,1)S(1)}, u32[]{:S(2)}, u32[]{:S(2)}) collective-permute-start(bf16[4,2,128,128]{3,2,1,0:T(8,128)(2,1)S(1)} %collective-permute-done.7.refs_4_), channel_id=1, source_target_pairs={{0,4},{4,8},{8,12},{12,14},{14,10},{10,6},{6,2},{2,0},{1,3},{5,1},... | collective-permute-start | bytes 786440 | tf_op jit(solution)/shard_map/ppermute | solution.py:188
  14.8 6.4 %collective-permute-start.2 = (bf16[4,2,128,128]{3,2,1,0:T(8,128)(2,1)S(1)}, bf16[4,2,128,128]{3,2,1,0:T(8,128)(2,1)S(1)}, u32[]{:S(2)}, u32[]{:S(2)}) collective-permute-start(bf16[4,2,128,128]{3,2,1,0:T(8,128)(2,1)S(1)} %collective-permute-done.1.refs_0_), channel_id=1, source_target_pairs={{0,4},{4,8},{8,12},{12,14},{14,10},{10,6},{6,2},{2,0},{1,3},{5,1},... | collective-permute-start | bytes 786440 | tf_op jit(solution)/shard_map/ppermute | solution.py:188
  16.9 6.4 %collective-permute-start.13 = (bf16[4,2,128,128]{3,2,1,0:T(8,128)(2,1)S(1)}, bf16[4,2,128,128]{3,2,1,0:T(8,128)(2,1)S(1)}, u32[]{:S(2)}, u32[]{:S(2)}) collective-permute-start(bf16[4,2,128,128]{3,2,1,0:T(8,128)(2,1)S(1)} %collective-permute-done.refs_2_), channel_id=1, source_target_pairs={{0,1},{1,0},{2,3},{3,2},{4,5},{5,4},{6,7},{7,6},{8,9},{9,8},{10,11... | collective-permute-start | bytes 786440 | tf_op jit(solution)/shard_map/ppermute | solution.py:189
  16.9 6.9 %collective-permute-start.14 = (bf16[4,2,128,128]{3,2,1,0:T(8,128)(2,1)S(1)}, bf16[4,2,128,128]{3,2,1,0:T(8,128)(2,1)S(1)}, u32[]{:S(2)}, u32[]{:S(2)}) collective-permute-start(bf16[4,2,128,128]{3,2,1,0:T(8,128)(2,1)S(1)} %collective-permute-done.7.refs_4_), channel_id=1, source_target_pairs={{0,1},{1,0},{2,3},{3,2},{4,5},{5,4},{6,7},{7,6},{8,9},{9,8},{10,11... | collective-permute-start | bytes 786440 | tf_op jit(solution)/shard_map/ppermute | solution.py:189
  17.6 6.4 %collective-permute-start.9 = (bf16[4,2,128,128]{3,2,1,0:T(8,128)(2,1)S(1)}, bf16[4,2,128,128]{3,2,1,0:T(8,128)(2,1)S(1)}, u32[]{:S(2)}, u32[]{:S(2)}) collective-permute-start(bf16[4,2,128,128]{3,2,1,0:T(8,128)(2,1)S(1)} %collective-permute-done.8.refs_2_), channel_id=1, source_target_pairs={{0,4},{4,8},{8,12},{12,14},{14,10},{10,6},{6,2},{2,0},{1,3},{5,1},... | collective-permute-start | bytes 786440 | tf_op jit(solution)/shard_map/ppermute | solution.py:188
  21.2 6.4 %collective-permute-start.3 = (bf16[4,2,128,128]{3,2,1,0:T(8,128)(2,1)S(1)}, bf16[4,2,128,128]{3,2,1,0:T(8,128)(2,1)S(1)}, u32[]{:S(2)}, u32[]{:S(2)}) collective-permute-start(bf16[4,2,128,128]{3,2,1,0:T(8,128)(2,1)S(1)} %collective-permute-done.2.refs_0_), channel_id=1, source_target_pairs={{0,4},{4,8},{8,12},{12,14},{14,10},{10,6},{6,2},{2,0},{1,3},{5,1},... | collective-permute-start | bytes 786440 | tf_op jit(solution)/shard_map/ppermute | solution.py:188
  23.3 17.6 %collective-permute-start.11 = (bf16[4,2,128,128]{3,2,1,0:T(8,128)(2,1)S(1)}, bf16[4,2,128,128]{3,2,1,0:T(8,128)(2,1)S(1)}, u32[]{:S(2)}, u32[]{:S(2)}) collective-permute-start(bf16[4,2,128,128]{3,2,1,0:T(8,128)(2,1)S(1)} %collective-permute-done.1.refs_0_), channel_id=1, source_target_pairs={{0,1},{1,0},{2,3},{3,2},{4,5},{5,4},{6,7},{7,6},{8,9},{9,8},{10,11... | collective-permute-start | bytes 786440 | tf_op jit(solution)/shard_map/ppermute | solution.py:189
  23.3 17.6 %collective-permute-start.12 = (bf16[4,2,128,128]{3,2,1,0:T(8,128)(2,1)S(1)}, bf16[4,2,128,128]{3,2,1,0:T(8,128)(2,1)S(1)}, u32[]{:S(2)}, u32[]{:S(2)}) collective-permute-start(bf16[4,2,128,128]{3,2,1,0:T(8,128)(2,1)S(1)} %collective-permute-done.8.refs_2_), channel_id=1, source_target_pairs={{0,1},{1,0},{2,3},{3,2},{4,5},{5,4},{6,7},{7,6},{8,9},{9,8},{10,11... | collective-permute-start | bytes 786440 | tf_op jit(solution)/shard_map/ppermute | solution.py:189
  23.8 19.1 %collective-permute-start.5 = (bf16[4,2,128,128]{3,2,1,0:T(8,128)(2,1)S(1)}, bf16[4,2,128,128]{3,2,1,0:T(8,128)(2,1)S(1)}, u32[]{:S(2)}, u32[]{:S(2)}) collective-permute-start(bf16[4,2,128,128]{3,2,1,0:T(8,128)(2,1)S(1)} %collective-permute-done.2.refs_0_), channel_id=1, source_target_pairs={{0,1},{1,0},{2,3},{3,2},{4,5},{5,4},{6,7},{7,6},{8,9},{9,8},{10,11... | collective-permute-start | bytes 786440 | tf_op jit(solution)/shard_map/ppermute | solution.py:189
  24.0 18.9 %collective-permute-start.10 = (bf16[4,2,128,128]{3,2,1,0:T(8,128)(2,1)S(1)}, bf16[4,2,128,128]{3,2,1,0:T(8,128)(2,1)S(1)}, u32[]{:S(2)}, u32[]{:S(2)}) collective-permute-start(bf16[4,2,128,128]{3,2,1,0:T(8,128)(2,1)S(1)} %collective-permute-done.9.refs_2_), channel_id=1, source_target_pairs={{0,1},{1,0},{2,3},{3,2},{4,5},{5,4},{6,7},{7,6},{8,9},{9,8},{10,11... | collective-permute-start | bytes 786440 | tf_op jit(solution)/shard_map/ppermute | solution.py:189
  27.6 17.3 %collective-permute-start.4 = (bf16[4,2,128,128]{3,2,1,0:T(8,128)(2,1)S(1)}, bf16[4,2,128,128]{3,2,1,0:T(8,128)(2,1)S(1)}, u32[]{:S(2)}, u32[]{:S(2)}) collective-permute-start(bf16[4,2,128,128]{3,2,1,0:T(8,128)(2,1)S(1)} %collective-permute-done.3.refs_0_), channel_id=1, source_target_pairs={{0,1},{1,0},{2,3},{3,2},{4,5},{5,4},{6,7},{7,6},{8,9},{9,8},{10,11... | collective-permute-start | bytes 786440 | tf_op jit(solution)/shard_map/ppermute | solution.py:189
  28.3 2.2 %copy-start = (bf16[16,8,128,128]{3,2,1,0:T(8,128)(2,1)S(1)}, bf16[16,8,128,128]{3,2,1,0:T(8,128)(2,1)}, u32[]{:S(2)}) copy-start(bf16[16,8,128,128]{3,2,1,0:T(8,128)(2,1)} %wave_ref.1) | copy-start | bytes 12582916
  30.5 1.2 %copy-start.1 = (bf16[16,2,128,128]{3,2,1,0:T(8,128)(2,1)S(1)}, bf16[16,2,128,128]{3,2,1,0:T(8,128)(2,1)}, u32[]{:S(2)}) copy-start(bf16[16,2,128,128]{3,2,1,0:T(8,128)(2,1)} %left_ref.1) | copy-start | bytes 3145732
  31.7 0.7 %copy-start.2 = (s32[16,8]{0,1:T(8,128)S(1)}, s32[16,8]{0,1:T(8,128)}, u32[]{:S(2)}) copy-start(s32[16,8]{0,1:T(8,128)} %param.13) | copy-start | bytes 1540
  32.4 0.7 %copy-start.3 = (s32[16,8]{0,1:T(8,128)S(1)}, s32[16,8]{0,1:T(8,128)}, u32[]{:S(2)}) copy-start(s32[16,8]{0,1:T(8,128)} %param.14) | copy-start | bytes 1540
  33.1 0.7 %copy-start.4 = (s32[16]{0:T(128)S(1)}, s32[16]{0:T(128)}, u32[]{:S(2)}) copy-start(s32[16]{0:T(128)} %length_ref.2) | copy-start | bytes 196

commit v2 on v0

v2 whole, which is shorter than its diff:
```python
import functools

import jax
import jax.numpy as jnp
from jax import lax
from jax.experimental import pallas as pl
from jax.experimental.pallas import tpu as pltpu
from jax.sharding import PartitionSpec as P

SMEM = pl.BlockSpec(memory_space=pltpu.SMEM)
VMEM = pl.BlockSpec(memory_space=pltpu.VMEM)
ANY = pl.BlockSpec(memory_space=pl.ANY)
TOKEN = (8, 128)
GROUP = 2
PACE = 1150000000
LIMIT = pltpu.CompilerParams(vmem_limit_bytes=16 << 20)


def live(size, length):
    rows = lax.broadcasted_iota(jnp.int32, (size, size), 0)
    columns = lax.broadcasted_iota(jnp.int32, (size, size), 1)
    return (rows < length) & (columns < length)


def vmem(x):
    return pltpu.with_memory_space_constraint(x, pltpu.VMEM)


def hbm(x):
    return pltpu.with_memory_space_constraint(x, pltpu.HBM)


def mask_kernel(length_hbm, blocks_hbm, out_ref, length_ref, blocks_ref, sems):
    sectors, terms, size, _ = blocks_ref.shape
    lengths = pltpu.make_async_copy(length_hbm, length_ref, sems.at[sectors])
    blocks = [pltpu.make_async_copy(blocks_hbm.at[b], blocks_ref.at[b], sems.at[b]) for b in range(sectors)]
    lengths.start()
    for copy in blocks:
        copy.start()
    lengths.wait()
    for b in range(sectors):
        keep = live(size, length_ref[b])
        blocks[b].wait()
        for k in range(terms):
            block = blocks_ref[b, k]
            out_ref[b, k] = jnp.where(keep, block, jnp.zeros_like(block))


def mask_right(lengths, blocks):
    return pl.pallas_call(
        mask_kernel,
        in_specs=[ANY, ANY],
        out_specs=VMEM,
        out_shape=pltpu.VMEM(blocks.shape, blocks.dtype),
        scratch_shapes=[
            pltpu.SMEM(lengths.shape, jnp.int32),
            pltpu.VMEM(blocks.shape, blocks.dtype),
            pltpu.SemaphoreType.DMA((blocks.shape[0] + 1,)),
        ],
        compiler_params=pltpu.CompilerParams(vmem_limit_bytes=2 << 20),
        name="mask_right",
    )(hbm(lengths), hbm(blocks))


def join_kernel(block_ref, token_ref, out_ref):
    del block_ref, token_ref, out_ref


def join(block, token):
    return pl.pallas_call(
        join_kernel,
        in_specs=[VMEM, VMEM],
        out_specs=VMEM,
        out_shape=pltpu.VMEM(block.shape, block.dtype),
        input_output_aliases={0: 0},
        compiler_params=pltpu.CompilerParams(vmem_limit_bytes=1 << 20),
        name="join",
    )(vmem(block), vmem(token))


def multiply_left(low, high, length_ref, left_ref, wave_ref, partial_ref, ready=lambda a: None):
    terms, size = left_ref.shape[1:3]
    partners = wave_ref.shape[1]
    for a in range(low, high):
        ready(a)
        keep = live(size, length_ref[a])
        left = jnp.concatenate([jnp.where(keep, left_ref[a, k], 0) for k in range(terms)], axis=0)
        for j in range(0, partners, 2):
            wave = jnp.concatenate([wave_ref[a, j], wave_ref[a, j + 1]], axis=1)
            both = jnp.dot(left, wave, preferred_element_type=jnp.float32).astype(partial_ref.dtype)
            for i in range(2):
                for k in range(terms):
                    partial_ref[a * partners + j + i, :, k * size:(k + 1) * size] = (
                        both[k * size:(k + 1) * size, i * size:(i + 1) * size])


def opening_kernel(high, cap, slots, origins, length_hbm, owner_hbm, slot_hbm, left_hbm, wave_hbm,
                   partial_ref, token_ref, work_ref, count_ref, length_ref, left_ref, wave_ref,
                   owner_ref, slot_ref, place_ref, sems, scalar_sems):
    sectors, partners = wave_hbm.shape[:2]
    scalars = [
        pltpu.make_async_copy(source, target, scalar_sems.at[i])
        for i, (source, target) in enumerate(((length_hbm, length_ref), (owner_hbm, owner_ref), (slot_hbm, slot_ref)))]
    arrays = []
    for g in range(sectors // GROUP):
        at = pl.ds(g * GROUP, GROUP)
        arrays.append([
            pltpu.make_async_copy(left_hbm.at[at], left_ref.at[at], sems.at[0, g]),
            pltpu.make_async_copy(wave_hbm.at[at], wave_ref.at[at], sems.at[1, g])])
    for copy in scalars + sum(arrays, []):
        copy.start()
    token_ref[...] = jnp.zeros_like(token_ref)
    for c, origin in enumerate(origins(lax.axis_index("sect"))):
        place_ref[origin] = c
        count_ref[c] = 0
    for copy in scalars:
        copy.wait()
    for a in range(sectors):
        for j in range(partners):
            chunk = place_ref[owner_ref[j, a]]
            filled = count_ref[chunk]
            count_ref[chunk] = filled + 1
            work_ref[chunk * cap + filled] = (a * partners + j) * slots + slot_ref[j, a]

    def ready(a):
        if a % GROUP == 0:
            for copy in arrays[a // GROUP]:
                copy.wait()

    multiply_left(0, high, length_ref, left_ref, wave_ref, partial_ref, ready)
    for a in range(high, sectors):
        ready(a)


def opening(high, n, cap, slots, origins, lengths, owner, slot, left, wave):
    sectors, partners, size, _ = wave.shape
    terms = left.shape[1]
    return pl.pallas_call(
        functools.partial(opening_kernel, high, cap, slots, origins),
        in_specs=[ANY] * 5,
        out_specs=[VMEM, VMEM, SMEM, SMEM, SMEM, VMEM, VMEM],
        out_shape=[
            pltpu.VMEM((sectors * partners, size, terms * size), wave.dtype),
            pltpu.VMEM(TOKEN, jnp.float32),
            pltpu.SMEM((n * cap,), jnp.int32),
            pltpu.SMEM((n,), jnp.int32),
            pltpu.SMEM(lengths.shape, jnp.int32),
            pltpu.VMEM(left.shape, left.dtype),
            pltpu.VMEM(wave.shape, wave.dtype),
        ],
        scratch_shapes=[
            pltpu.SMEM(owner.shape, jnp.int32),
            pltpu.SMEM(slot.shape, jnp.int32),
            pltpu.SMEM((n,), jnp.int32),
            pltpu.SemaphoreType.DMA((2, sectors // GROUP)),
            pltpu.SemaphoreType.DMA((3,)),
        ],
        compiler_params=LIMIT,
        cost_estimate=pl.CostEstimate(flops=PACE, bytes_accessed=0, transcendentals=0),
        name="opening",
    )(*map(hbm, (lengths, owner, slot, left, wave)))


def partial_kernel(low, high, length_ref, left_ref, wave_ref, _, partial_ref, token_ref):
    token_ref[...] = jnp.zeros_like(token_ref)
    multiply_left(low, high, length_ref, left_ref, wave_ref, partial_ref)


def partials(low, high, lengths, left, wave, before):
    return pl.pallas_call(
        functools.partial(partial_kernel, low, high),
        in_specs=[SMEM, VMEM, VMEM, VMEM],
        out_specs=[VMEM, VMEM],
        out_shape=[pltpu.VMEM(before.shape, before.dtype), pltpu.VMEM(TOKEN, jnp.float32)],
        input_output_aliases={3: 0},
        compiler_params=LIMIT,
        cost_estimate=pl.CostEstimate(flops=PACE, bytes_accessed=0, transcendentals=0),
        name="partials",
    )(lengths, vmem(left), vmem(wave), vmem(before))


def product_kernel(first, cap, exact, chunks, flush, given, marked, work_ref, count_ref, partial_ref, *refs):
    right_refs, refs = refs[:chunks], refs[chunks:]
    refs = refs[given:]
    stage, refs = refs[0], refs[1:]
    slots, terms = right_refs[0].shape[:2]
    if marked:
        refs[0][...] = jnp.zeros_like(refs[0])
        refs = refs[1:]

    def each(low, high, body):
        for c in range(low, high):
            for i in range(cap):
                if exact:
                    body(c, i)
                else:
                    pl.when(i < count_ref[c])(functools.partial(body, c, i))

    def where(c, i):
        entry = work_ref[c * cap + i]
        return lax.div(entry, slots), lax.rem(entry, slots)

    def item(c, i):
        index, slot = where(c, i)
        right = jnp.concatenate([right_refs[c - first][slot, k] for k in range(terms)], axis=1)
        stage[index] = lax.dot_general(
            partial_ref[index], right, (((1,), (1,)), ((), ())), preferred_element_type=jnp.float32,
        ).astype(stage.dtype)

    if flush is None:
        each(first, first + chunks, item)
        return
    out_ref, sem = refs

    def copy(c, i):
        index, _ = where(c, i)
        return pltpu.make_async_copy(stage.at[index], out_ref.at[index], sem)

    def start(c, i):
        copy(c, i).start()

    def both(c, i):
        item(c, i)
        start(c, i)

    each(flush, first, start)
    each(first, first + chunks, both)
    if exact:
        whole = out_ref.at[pl.ds(0, (first + chunks - flush) * cap)]
        pltpu.make_async_copy(whole, whole, sem).wait()
    else:
        each(flush, first + chunks, lambda c, i: copy(c, i).wait())


def products(first, cap, exact, flush, marked, work, count, partial_value, rights, stage, out):
    blocks, size, _ = partial_value.shape
    chunks = len(rights)
    operands = [vmem(stage)] if stage is not None else []
    specs = [VMEM] * len(operands)
    aliases = {3 + chunks: 0} if operands else {}
    out_specs, out_shape, scratch = [VMEM], [pltpu.VMEM((blocks, size, size), partial_value.dtype)], []
    if marked:
        out_specs.append(VMEM)
        out_shape.append(pltpu.VMEM(TOKEN, jnp.float32))
    if flush is not None:
        out_specs.append(ANY)
        out_shape.append(jax.ShapeDtypeStruct((blocks, size, size), partial_value.dtype))
        scratch.append(pltpu.SemaphoreType.DMA)
        if out is not None:
            aliases[3 + chunks + len(operands)] = 1 + marked
            operands.append(out)
            specs.append(ANY)
    result = pl.pallas_call(
        functools.partial(product_kernel, first, cap, exact, chunks, flush, len(operands), marked),
        in_specs=[SMEM, SMEM, VMEM] + [VMEM] * chunks + specs,
        out_specs=out_specs,
        out_shape=out_shape,
        scratch_shapes=scratch,
        input_output_aliases=aliases,
        compiler_params=LIMIT,
        cost_estimate=pl.CostEstimate(flops=PACE, bytes_accessed=0, transcendentals=0),
        name="products",
    )(work, count, vmem(partial_value), *map(vmem, rights), *operands)
    stage, *result = result
    token = result.pop(0) if marked else None
    return stage, token, result[0] if result else out


def local(n, wavefunction, left_environment, right_environment, left_length, right_length, right_owner, right_slot):
    sectors, partners = wavefunction.shape[:2]
    blocks = sectors * partners
    cap = max(2, blocks // n)
    exact = cap * n == blocks
    chips = n // 2
    hops = chips // 2

    def chip_at(i):
        i = i % chips
        return 2 * i if i < hops else 2 * (chips - 1 - i) + 1

    onward = [(chip_at(i) * 2, chip_at(i + 1) * 2) for i in range(chips)]
    onward += [(chip_at(i) * 2 + 1, chip_at(i - 1) * 2 + 1) for i in range(chips)]
    across = [(d, d ^ 1) for d in range(n)]

    plan = [(0, 0, 0), (0, 1, 0)]
    for hop in range(1, hops + 1):
        plan += [(hop, 0, 0), (hop, 0, 1)]
        if hop < hops:
            plan += [(hop, 1, 0), (hop, 1, 1)]

    def origins(device):
        core, chip = lax.rem(device, 2), lax.div(device, 2)
        half = lax.div(chip, 2)
        at = jnp.where(lax.rem(chip, 2) == 0, half, chips - 1 - half)
        for hop, other, via in plan:
            carrier = core if via == 0 else 1 - core
            i = lax.rem(at + jnp.where(carrier == 0, chips - hop, hop), chips)
            source = jnp.where(i < hops, 2 * i, 2 * (chips - 1 - i) + 1)
            yield 2 * source + (carrier if other == 0 else 1 - carrier)

    def send(block, perm):
        return lax.ppermute(block, "sect", perm)

    first = mask_right(right_length, right_environment)
    held = {(0, 0, 0): first, (1, 0, 0): send(first, onward)}
    held[0, 1, 0] = send(first, across)
    held[1, 1, 0] = send(held[0, 1, 0], onward)
    part = work = count = stage = out = None
    cuts = [sectors // 2, 3 * sectors // 4, sectors]
    done = 0
    windows = [(hop, other) for hop in range(1, hops + 1) for other in (0, 1) if hop < hops or not other]
    for at, (hop, other) in enumerate(windows):
        if not at:
            part, token, work, count, lengths, left, wave = opening(
                cuts[0], n, cap, right_environment.shape[0], origins, left_length, right_owner.T, right_slot.T, left_environment, wavefunction)
        elif at < len(cuts):
            part, token = partials(cuts[at - 1], cuts[at], lengths, left, wave, part)
        else:
            upto = 2 * at if at + 1 < len(windows) else 2 * at + 1
            stage, token, out = products(
                done, cap, exact, 0 if at + 1 == len(windows) else None, True, work, count, part,
                [held[p] for p in plan[done:upto]], stage, out)
            done = upto
        here = held[hop, other, 0] = join(held[hop, other, 0], token)
        if hop + 1 + other <= hops:
            held[hop + 1, other, 0] = send(here, onward)
        held[hop, other, 1] = send(here, across)
    flushed = done
    for upto in (n - 1, n):
        stage, token, out = products(
            done, cap, exact, flushed, False, work, count, part, [held[p] for p in plan[done:upto]], stage, out)
        done = flushed = upto
    return out.reshape(wavefunction.shape)


def solution(mesh):
    split = ("groups", "sect")
    return jax.shard_map(
        functools.partial(local, mesh.shape["sect"]),
        mesh=mesh,
        in_specs=(
            P(split, None, None, None),
            P(split, None, None, None),
            P(split, None, None, None),
            P(split),
            P(split),
            P(split, None),
            P(split, None),
        ),
        out_specs=P(split, None, None, None),
        check_vma=False,
    )
```

time: 87.5 us -> 31 us (0.35)
  waiting for transfers between devices: 51.6 us -> 6.17 us
  between operations: 13.4 us -> 0.13 us
  starting transfers between devices: 0.01 us -> 13.1 us
  Pallas kernels: 0 us -> 11.5 us
  local copies, waits for them, and re-layouts: 8.98 us -> 0 us
  matrix products: 8.84 us -> 0 us
  other arithmetic: 4.34 us -> 0 us
    all_gather x1 -> x0, waiting for transfers between devices: 51.6 us -> none  [local(): everyone = lax.all_gather(right_live, 'sect', axis=0, tiled=True)]
    ppermute x0 -> x15, starting transfers between devices: none -> 13.1 us  [send(): return lax.ppermute(block, 'sect', perm)]
    pallas_call x0 -> x17, Pallas kernels: none -> 11.5 us  [the longest x6 5.65 us: products(): pl.pallas_call(functools.partial(product_kernel, first, cap, exact, chunk...]
    dot_general x1 -> x0, matrix products: 8.84 us -> none  [local(): jnp.einsum('ajkpr,ajkcr->ajpc', partial_value, chosen, preferred_element_...]
    gather x1 -> x0, local copies, waits for them, and re-layouts: 8.73 us -> none  [local(): jnp.take(everyone, destination, axis=0)]
    ppermute x0 -> x15, waiting for transfers between devices: none -> 6.17 us  [send(): return lax.ppermute(block, 'sect', perm)]
    select_n x2 -> x0, other arithmetic: 1.68 us -> none  [the longest x1 1.68 us: mask_blocks(): return jnp.where(keep[:, None, :, :], blocks, jnp.zeros_like(blocks))]
    lt x2 -> x0, other arithmetic: 1.46 us -> none  [mask_blocks(): live_rows = indices[None, :] < lengths[:, None]]
  transfers between devices with their start and end apart: 1 -> 15, of which waited for: 1 -> 6; matrix products, arithmetic and copies ran while one was open for 2% -> 0% of each run, Pallas kernels for 0% -> 31%
where the time goes in v2:
time: 31 us; the launch traced here: 30.9 us
  starting transfers between devices  13.1 us (42%)
  Pallas kernels  11.5 us (37%)
  waiting for transfers between devices  6.17 us (20%)
    ppermute x15, starting transfers between devices, send(): return lax.ppermute(block, 'sect', perm)  13.1 us
    ppermute x15, waiting for transfers between devices, send(): return lax.ppermute(block, 'sect', perm)  6.17 us
    pallas_call x6, Pallas kernels, products(): pl.pallas_call(functools.partial(product_kernel, first, cap, exact, chunk...  5.65 us
    pallas_call x1, Pallas kernels, opening(): pl.pallas_call(functools.partial(opening_kernel, high, cap, slots, origin...  3.43 us
    pallas_call x2, Pallas kernels, partials(): pl.pallas_call(functools.partial(partial_kernel, low, high), in_specs=[SM...  1.38 us
    pallas_call x1, Pallas kernels, mask_right(): pl.pallas_call(mask_kernel, in_specs=[ANY, ANY], out_specs=VMEM, out_shap...  1 us
  transfers between devices with their start and end apart: 15, of which 6 were waited for; matrix products, arithmetic and copies ran while one was open for 0% of the time, Pallas kernels for 31%

profile of v2, /device:TPU:0, one launch (start us, length us, event | category | flops | bytes accessed | tf_op | source)
XLA Modules:
  0.0 30.9 jit_solution(15251523209156296800)
XLA Ops:
  0.0 1.0 %mask_right.1.refs_0_ = bf16[4,2,128,128]{3,2,1,0:T(8,128)(2,1)S(1)} custom-call(s32[4]{0:T(128)} %length_hbm.3, bf16[4,2,128,128]{3,2,1,0:T(8,128)(2,1)} %blocks_hbm.1), custom_call_target="tpu_custom_call" | custom-call | tf_op jit(solution)/shard_map/mask_right/pallas_call | solution.py:50
  1.0 0.5 %collective-permute-start.4 = (bf16[4,2,128,128]{3,2,1,0:T(8,128)(2,1)S(1)}, bf16[4,2,128,128]{3,2,1,0:T(8,128)(2,1)S(1)}, u32[]{:S(2)}, u32[]{:S(2)}) collective-permute-start(bf16[4,2,128,128]{3,2,1,0:T(8,128)(2,1)S(1)} %mask_right.1.refs_0_), channel_id=1, source_target_pairs={{0,1},{1,0},{2,3},{3,2},{4,5},{5,4},{6,7},{7,6},{8,9},{9,8},{10,11... | collective-permute-start | bytes 786440 | tf_op jit(solution)/shard_map/ppermute | solution.py:302
  1.5 2.6 %collective-permute-start = (bf16[4,2,128,128]{3,2,1,0:T(8,128)(2,1)S(1)}, bf16[4,2,128,128]{3,2,1,0:T(8,128)(2,1)S(1)}, u32[]{:S(2)}, u32[]{:S(2)}) collective-permute-start(bf16[4,2,128,128]{3,2,1,0:T(8,128)(2,1)S(1)} %mask_right.1.refs_0_), channel_id=1, source_target_pairs={{0,4},{4,8},{8,12},{12,14},{14,10},{10,6},{6,2},{2,0},{1,3},{5,1},... | collective-permute-start | bytes 786440 | tf_op jit(solution)/shard_map/ppermute | solution.py:302
  4.2 1.6 %collective-permute-start.6 = (bf16[4,2,128,128]{3,2,1,0:T(8,128)(2,1)S(1)}, bf16[4,2,128,128]{3,2,1,0:T(8,128)(2,1)S(1)}, u32[]{:S(2)}, u32[]{:S(2)}) collective-permute-start(bf16[4,2,128,128]{3,2,1,0:T(8,128)(2,1)S(1)} %collective-permute-done.4.refs_1_), channel_id=1, source_target_pairs={{0,4},{4,8},{8,12},{12,14},{14,10},{10,6},{6,2},{2,0},{1,3},{5,1},... | collective-permute-start | bytes 786440 | tf_op jit(solution)/shard_map/ppermute | solution.py:302
  5.7 3.4 %opening.1 = (bf16[128,128,256]{2,1,0:T(8,128)(2,1)S(1)}, f32[8,128]{1,0:T(8,128)S(1)}, s32[128]{0:T(128)S(4)}, s32[16]{0:T(128)S(4)}, s32[16]{0:T(128)S(4)}, /*...) custom-call(s32[16]{0:T(128)} %length_hbm.2, s32[8,16]{1,0:T(8,128)} %bitcast.3, ...), custom_call_target="tpu_custom_call" | custom-call | flops 1150000000 | tf_op jit(solution)/shard_map/opening/pallas_call | solution.py:138
  9.2 1.6 %collective-permute-start.1 = (bf16[4,2,128,128]{3,2,1,0:T(8,128)(2,1)S(1)}, bf16[4,2,128,128]{3,2,1,0:T(8,128)(2,1)S(1)}, u32[]{:S(2)}, u32[]{:S(2)}) collective-permute-start(bf16[4,2,128,128]{3,2,1,0:T(8,128)(2,1)S(1)} %join.7.refs_2_), channel_id=1, source_target_pairs={{0,4},{4,8},{8,12},{12,14},{14,10},{10,6},{6,2},{2,0},{1,3},{5,1},... | collective-permute-start | bytes 786440 | tf_op jit(solution)/shard_map/ppermute | solution.py:302
  10.8 0.7 %partials.2 = (bf16[128,128,256]{2,1,0:T(8,128)(2,1)S(1)}, f32[8,128]{1,0:T(8,128)S(1)}) custom-call(s32[16]{0:T(128)S(4)} %get-tuple-element.30.length_ref, bf16[16,2,128,128]{3,2,1,0:T(8,128)(2,1)S(1)} %get-tuple-element.31.left_ref, bf16[16,8,128,128]{3,2,1,0:T(8,128)(2,1)S(1)} %get-tuple-element.32.wave_ref, ...), custom_call_target="tpu_custom_call", output_to_operand_aliasing={{0}: (3, {})} | custom-call | flops 1150000000 | tf_op jit(solution)/shard_map/partials/pallas_call | solution.py:170
  11.6 0.5 %collective-permute-start.7 = (bf16[4,2,128,128]{3,2,1,0:T(8,128)(2,1)S(1)}, bf16[4,2,128,128]{3,2,1,0:T(8,128)(2,1)S(1)}, u32[]{:S(2)}, u32[]{:S(2)}) collective-permute-start(bf16[4,2,128,128]{3,2,1,0:T(8,128)(2,1)S(1)} %join.9.refs_4_), channel_id=1, source_target_pairs={{0,1},{1,0},{2,3},{3,2},{4,5},{5,4},{6,7},{7,6},{8,9},{9,8},{10,11... | collective-permute-start | bytes 786440 | tf_op jit(solution)/shard_map/ppermute | solution.py:302
  12.1 1.5 %collective-permute-start.10 = (bf16[4,2,128,128]{3,2,1,0:T(8,128)(2,1)S(1)}, bf16[4,2,128,128]{3,2,1,0:T(8,128)(2,1)S(1)}, u32[]{:S(2)}, u32[]{:S(2)}) collective-permute-start(bf16[4,2,128,128]{3,2,1,0:T(8,128)(2,1)S(1)} %join.9.refs_4_), channel_id=1, source_target_pairs={{0,4},{4,8},{8,12},{12,14},{14,10},{10,6},{6,2},{2,0},{1,3},{5,1},... | collective-permute-start | bytes 786440 | tf_op jit(solution)/shard_map/ppermute | solution.py:302
  13.6 0.7 %partials.3 = (bf16[128,128,256]{2,1,0:T(8,128)(2,1)S(1)}, f32[8,128]{1,0:T(8,128)S(1)}) custom-call(s32[16]{0:T(128)S(4)} %get-tuple-element.30.length_ref, bf16[16,2,128,128]{3,2,1,0:T(8,128)(2,1)S(1)} %get-tuple-element.31.left_ref, bf16[16,8,128,128]{3,2,1,0:T(8,128)(2,1)S(1)} %get-tuple-element.32.wave_ref, ...), custom_call_target="tpu_custom_call", output_to_operand_aliasing={{0}: (3, {})} | custom-call | flops 1150000000 | tf_op jit(solution)/shard_map/partials/pallas_call | solution.py:170
  14.3 1.3 %collective-permute-done.1.block_ref = bf16[4,2,128,128]{3,2,1,0:T(8,128)(2,1)S(1)} collective-permute-done((bf16[4,2,128,128]{3,2,1,0:T(8,128)(2,1)S(1)}, bf16[4,2,128,128]{3,2,1,0:T(8,128)(2,1)S(1)}, u32[]{:S(2)}, u32[]{:S(2)}) %collective-permute-start.1) | collective-permute-done | bytes 262176 | tf_op jit(solution)/shard_map/ppermute | solution.py:302
  15.6 1.6 %collective-permute-start.2 = (bf16[4,2,128,128]{3,2,1,0:T(8,128)(2,1)S(1)}, bf16[4,2,128,128]{3,2,1,0:T(8,128)(2,1)S(1)}, u32[]{:S(2)}, u32[]{:S(2)}) collective-permute-start(bf16[4,2,128,128]{3,2,1,0:T(8,128)(2,1)S(1)} %join.8.refs_0_), channel_id=1, source_target_pairs={{0,4},{4,8},{8,12},{12,14},{14,10},{10,6},{6,2},{2,0},{1,3},{5,1},... | collective-permute-start | bytes 786440 | tf_op jit(solution)/shard_map/ppermute | solution.py:302
  17.2 1.0 %products.6 = (bf16[128,128,128]{2,1,0:T(8,128)(2,1)S(1)}, f32[8,128]{1,0:T(8,128)S(1)}) custom-call(s32[128]{0:T(128)S(4)} %get-tuple-element.28.work_ref, s32[16]{0:T(128)S(4)} %get-tuple-element.29.count_ref, bf16[128,128,256]{2,1,0:T(8,128)(2,1)S(1)} %get-tuple-element.35.partial_ref, bf16[4,2,128,128]{3,2,1,0:T(8,128)(2,1)S(1)} %mask_right.1.refs_0_, ...), custom_call_target="tpu_custom_call" | custom-call | flops 1150000000 | tf_op jit(solution)/shard_map/products/pallas_call | solution.py:253
  18.5 1.5 %collective-permute-start.11 = (bf16[4,2,128,128]{3,2,1,0:T(8,128)(2,1)S(1)}, bf16[4,2,128,128]{3,2,1,0:T(8,128)(2,1)S(1)}, u32[]{:S(2)}, u32[]{:S(2)}) collective-permute-start(bf16[4,2,128,128]{3,2,1,0:T(8,128)(2,1)S(1)} %join.11.refs_0_), channel_id=1, source_target_pairs={{0,4},{4,8},{8,12},{12,14},{14,10},{10,6},{6,2},{2,0},{1,3},{5,1},... | collective-permute-start | bytes 786440 | tf_op jit(solution)/shard_map/ppermute | solution.py:302
  20.0 0.4 %products.7 = (bf16[128,128,128]{2,1,0:T(8,128)(2,1)S(1)}, f32[8,128]{1,0:T(8,128)S(1)}) custom-call(s32[128]{0:T(128)S(4)} %get-tuple-element.28.work_ref, s32[16]{0:T(128)S(4)} %get-tuple-element.29.count_ref, bf16[128,128,256]{2,1,0:T(8,128)(2,1)S(1)} %get-tuple-element.35.partial_ref, ...), custom_call_target="tpu_custom_call", output_to_operand_aliasing={{0}: (5, {})} | custom-call | flops 1150000000 | tf_op jit(solution)/shard_map/products/pallas_call | solution.py:253
  20.5 1.5 %collective-permute-done.2.block_ref = bf16[4,2,128,128]{3,2,1,0:T(8,128)(2,1)S(1)} collective-permute-done((bf16[4,2,128,128]{3,2,1,0:T(8,128)(2,1)S(1)}, bf16[4,2,128,128]{3,2,1,0:T(8,128)(2,1)S(1)}, u32[]{:S(2)}, u32[]{:S(2)}) %collective-permute-start.2) | collective-permute-done | bytes 262176 | tf_op jit(solution)/shard_map/ppermute | solution.py:302
  22.0 1.6 %collective-permute-start.8 = (bf16[4,2,128,128]{3,2,1,0:T(8,128)(2,1)S(1)}, bf16[4,2,128,128]{3,2,1,0:T(8,128)(2,1)S(1)}, u32[]{:S(2)}, u32[]{:S(2)}) collective-permute-start(bf16[4,2,128,128]{3,2,1,0:T(8,128)(2,1)S(1)} %join.10.refs_0_), channel_id=1, source_target_pairs={{0,4},{4,8},{8,12},{12,14},{14,10},{10,6},{6,2},{2,0},{1,3},{5,1},... | collective-permute-start | bytes 786440 | tf_op jit(solution)/shard_map/ppermute | solution.py:302
  23.6 0.4 %products.8 = (bf16[128,128,128]{2,1,0:T(8,128)(2,1)S(1)}, f32[8,128]{1,0:T(8,128)S(1)}) custom-call(s32[128]{0:T(128)S(4)} %get-tuple-element.28.work_ref, s32[16]{0:T(128)S(4)} %get-tuple-element.29.count_ref, bf16[128,128,256]{2,1,0:T(8,128)(2,1)S(1)} %get-tuple-element.35.partial_ref, ...), custom_call_target="tpu_custom_call", output_to_operand_aliasing={{0}: (5, {})} | custom-call | flops 1150000000 | tf_op jit(solution)/shard_map/products/pallas_call | solution.py:253
  24.0 0.8 %collective-permute-done.11.block_ref = bf16[4,2,128,128]{3,2,1,0:T(8,128)(2,1)S(1)} collective-permute-done((bf16[4,2,128,128]{3,2,1,0:T(8,128)(2,1)S(1)}, bf16[4,2,128,128]{3,2,1,0:T(8,128)(2,1)S(1)}, u32[]{:S(2)}, u32[]{:S(2)}) %collective-permute-start.11) | collective-permute-done | bytes 262176 | tf_op jit(solution)/shard_map/ppermute | solution.py:302
  24.9 1.7 %products.9 = (bf16[128,128,128]{2,1,0:T(8,128)(2,1)S(1)}, f32[8,128]{1,0:T(8,128)S(1)}, bf16[128,128,128]{2,1,0:T(8,128)(2,1)}) custom-call(s32[128]{0:T(128)S(4)} %get-tuple-element.28.work_ref, s32[16]{0:T(128)S(4)} %get-tuple-element.29.count_ref, bf16[128,128,256]{2,1,0:T(8,128)(2,1)S(1)} %get-tuple-element.35.partial_ref, ...), custom_call_target="tpu_custom_call", output_to_operand_aliasing={{0}: (6, {})} | custom-call | flops 1150000000 | tf_op jit(solution)/shard_map/products/pallas_call | solution.py:253
  26.6 1.8 %collective-permute-done.8.block_ref = bf16[4,2,128,128]{3,2,1,0:T(8,128)(2,1)S(1)} collective-permute-done((bf16[4,2,128,128]{3,2,1,0:T(8,128)(2,1)S(1)}, bf16[4,2,128,128]{3,2,1,0:T(8,128)(2,1)S(1)}, u32[]{:S(2)}, u32[]{:S(2)}) %collective-permute-start.8) | collective-permute-done | bytes 262176 | tf_op jit(solution)/shard_map/ppermute | solution.py:302
  28.4 1.1 %products.10 = (bf16[128,128,128]{2,1,0:T(8,128)(2,1)S(1)}, bf16[128,128,128]{2,1,0:T(8,128)(2,1)}) custom-call(s32[128]{0:T(128)S(4)} %get-tuple-element.28.work_ref, s32[16]{0:T(128)S(4)} %get-tuple-element.29.count_ref, bf16[128,128,256]{2,1,0:T(8,128)(2,1)S(1)} %get-tuple-element.35.partial_ref, ...), custom_call_target="tpu_custom_call", output_to_operand_aliasing={{0}: (5, {}), {1}: (6, {})} | custom-call | flops 1150000000 | tf_op jit(solution)/shard_map/products/pallas_call | solution.py:253
  29.5 0.4 %collective-permute-done.13.refs_0_ = bf16[4,2,128,128]{3,2,1,0:T(8,128)(2,1)S(1)} collective-permute-done((bf16[4,2,128,128]{3,2,1,0:T(8,128)(2,1)S(1)}, bf16[4,2,128,128]{3,2,1,0:T(8,128)(2,1)S(1)}, u32[]{:S(2)}, u32[]{:S(2)}) %collective-permute-start.13) | collective-permute-done | bytes 262176 | tf_op jit(solution)/shard_map/ppermute | solution.py:302
  29.9 0.9 %products.11 = (bf16[128,128,128]{2,1,0:T(8,128)(2,1)S(1)}, bf16[128,128,128]{2,1,0:T(8,128)(2,1)}) custom-call(s32[128]{0:T(128)S(4)} %get-tuple-element.28.work_ref, s32[16]{0:T(128)S(4)} %get-tuple-element.29.count_ref, bf16[128,128,256]{2,1,0:T(8,128)(2,1)S(1)} %get-tuple-element.35.partial_ref, ...), custom_call_target="tpu_custom_call", output_to_operand_aliasing={{0}: (4, {}), {1}: (5, {})} | custom-call | flops 1150000000 | tf_op jit(solution)/shard_map/products/pallas_call | solution.py:253
  (23 shorter events, 0.4 us)
Async XLA Ops:
  1.0 3.2 %collective-permute-start.4 = (bf16[4,2,128,128]{3,2,1,0:T(8,128)(2,1)S(1)}, bf16[4,2,128,128]{3,2,1,0:T(8,128)(2,1)S(1)}, u32[]{:S(2)}, u32[]{:S(2)}) collective-permute-start(bf16[4,2,128,128]{3,2,1,0:T(8,128)(2,1)S(1)} %mask_right.1.refs_0_), channel_id=1, source_target_pairs={{0,1},{1,0},{2,3},{3,2},{4,5},{5,4},{6,7},{7,6},{8,9},{9,8},{10,11... | collective-permute-start | bytes 786440 | tf_op jit(solution)/shard_map/ppermute | solution.py:302
  1.5 7.7 %collective-permute-start = (bf16[4,2,128,128]{3,2,1,0:T(8,128)(2,1)S(1)}, bf16[4,2,128,128]{3,2,1,0:T(8,128)(2,1)S(1)}, u32[]{:S(2)}, u32[]{:S(2)}) collective-permute-start(bf16[4,2,128,128]{3,2,1,0:T(8,128)(2,1)S(1)} %mask_right.1.refs_0_), channel_id=1, source_target_pairs={{0,4},{4,8},{8,12},{12,14},{14,10},{10,6},{6,2},{2,0},{1,3},{5,1},... | collective-permute-start | bytes 786440 | tf_op jit(solution)/shard_map/ppermute | solution.py:302
  4.2 7.4 %collective-permute-start.6 = (bf16[4,2,128,128]{3,2,1,0:T(8,128)(2,1)S(1)}, bf16[4,2,128,128]{3,2,1,0:T(8,128)(2,1)S(1)}, u32[]{:S(2)}, u32[]{:S(2)}) collective-permute-start(bf16[4,2,128,128]{3,2,1,0:T(8,128)(2,1)S(1)} %collective-permute-done.4.refs_1_), channel_id=1, source_target_pairs={{0,4},{4,8},{8,12},{12,14},{14,10},{10,6},{6,2},{2,0},{1,3},{5,1},... | collective-permute-start | bytes 786440 | tf_op jit(solution)/shard_map/ppermute | solution.py:302
  9.2 6.4 %collective-permute-start.1 = (bf16[4,2,128,128]{3,2,1,0:T(8,128)(2,1)S(1)}, bf16[4,2,128,128]{3,2,1,0:T(8,128)(2,1)S(1)}, u32[]{:S(2)}, u32[]{:S(2)}) collective-permute-start(bf16[4,2,128,128]{3,2,1,0:T(8,128)(2,1)S(1)} %join.7.refs_2_), channel_id=1, source_target_pairs={{0,4},{4,8},{8,12},{12,14},{14,10},{10,6},{6,2},{2,0},{1,3},{5,1},... | collective-permute-start | bytes 786440 | tf_op jit(solution)/shard_map/ppermute | solution.py:302
  11.5 5.7 %collective-permute-start.5 = (bf16[4,2,128,128]{3,2,1,0:T(8,128)(2,1)S(1)}, bf16[4,2,128,128]{3,2,1,0:T(8,128)(2,1)S(1)}, u32[]{:S(2)}, u32[]{:S(2)}) collective-permute-start(bf16[4,2,128,128]{3,2,1,0:T(8,128)(2,1)S(1)} %join.7.refs_2_), channel_id=1, source_target_pairs={{0,1},{1,0},{2,3},{3,2},{4,5},{5,4},{6,7},{7,6},{8,9},{9,8},{10,11... | collective-permute-start | bytes 786440 | tf_op jit(solution)/shard_map/ppermute | solution.py:302
  11.6 5.6 %collective-permute-start.7 = (bf16[4,2,128,128]{3,2,1,0:T(8,128)(2,1)S(1)}, bf16[4,2,128,128]{3,2,1,0:T(8,128)(2,1)S(1)}, u32[]{:S(2)}, u32[]{:S(2)}) collective-permute-start(bf16[4,2,128,128]{3,2,1,0:T(8,128)(2,1)S(1)} %join.9.refs_4_), channel_id=1, source_target_pairs={{0,1},{1,0},{2,3},{3,2},{4,5},{5,4},{6,7},{7,6},{8,9},{9,8},{10,11... | collective-permute-start | bytes 786440 | tf_op jit(solution)/shard_map/ppermute | solution.py:302
  12.1 6.4 %collective-permute-start.10 = (bf16[4,2,128,128]{3,2,1,0:T(8,128)(2,1)S(1)}, bf16[4,2,128,128]{3,2,1,0:T(8,128)(2,1)S(1)}, u32[]{:S(2)}, u32[]{:S(2)}) collective-permute-start(bf16[4,2,128,128]{3,2,1,0:T(8,128)(2,1)S(1)} %join.9.refs_4_), channel_id=1, source_target_pairs={{0,4},{4,8},{8,12},{12,14},{14,10},{10,6},{6,2},{2,0},{1,3},{5,1},... | collective-permute-start | bytes 786440 | tf_op jit(solution)/shard_map/ppermute | solution.py:302
  15.6 4.4 %collective-permute-start.3 = (bf16[4,2,128,128]{3,2,1,0:T(8,128)(2,1)S(1)}, bf16[4,2,128,128]{3,2,1,0:T(8,128)(2,1)S(1)}, u32[]{:S(2)}, u32[]{:S(2)}) collective-permute-start(bf16[4,2,128,128]{3,2,1,0:T(8,128)(2,1)S(1)} %join.8.refs_0_), channel_id=1, source_target_pairs={{0,1},{1,0},{2,3},{3,2},{4,5},{5,4},{6,7},{7,6},{8,9},{9,8},{10,11... | collective-permute-start | bytes 786440 | tf_op jit(solution)/shard_map/ppermute | solution.py:302
  15.6 6.4 %collective-permute-start.2 = (bf16[4,2,128,128]{3,2,1,0:T(8,128)(2,1)S(1)}, bf16[4,2,128,128]{3,2,1,0:T(8,128)(2,1)S(1)}, u32[]{:S(2)}, u32[]{:S(2)}) collective-permute-start(bf16[4,2,128,128]{3,2,1,0:T(8,128)(2,1)S(1)} %join.8.refs_0_), channel_id=1, source_target_pairs={{0,4},{4,8},{8,12},{12,14},{14,10},{10,6},{6,2},{2,0},{1,3},{5,1},... | collective-permute-start | bytes 786440 | tf_op jit(solution)/shard_map/ppermute | solution.py:302
  18.5 5.1 %collective-permute-start.12 = (bf16[4,2,128,128]{3,2,1,0:T(8,128)(2,1)S(1)}, bf16[4,2,128,128]{3,2,1,0:T(8,128)(2,1)S(1)}, u32[]{:S(2)}, u32[]{:S(2)}) collective-permute-start(bf16[4,2,128,128]{3,2,1,0:T(8,128)(2,1)S(1)} %join.11.refs_0_), channel_id=1, source_target_pairs={{0,1},{1,0},{2,3},{3,2},{4,5},{5,4},{6,7},{7,6},{8,9},{9,8},{10,11... | collective-permute-start | bytes 786440 | tf_op jit(solution)/shard_map/ppermute | solution.py:302
  18.5 6.4 %collective-permute-start.11 = (bf16[4,2,128,128]{3,2,1,0:T(8,128)(2,1)S(1)}, bf16[4,2,128,128]{3,2,1,0:T(8,128)(2,1)S(1)}, u32[]{:S(2)}, u32[]{:S(2)}) collective-permute-start(bf16[4,2,128,128]{3,2,1,0:T(8,128)(2,1)S(1)} %join.11.refs_0_), channel_id=1, source_target_pairs={{0,4},{4,8},{8,12},{12,14},{14,10},{10,6},{6,2},{2,0},{1,3},{5,1},... | collective-permute-start | bytes 786440 | tf_op jit(solution)/shard_map/ppermute | solution.py:302
  22.0 2.9 %collective-permute-start.9 = (bf16[4,2,128,128]{3,2,1,0:T(8,128)(2,1)S(1)}, bf16[4,2,128,128]{3,2,1,0:T(8,128)(2,1)S(1)}, u32[]{:S(2)}, u32[]{:S(2)}) collective-permute-start(bf16[4,2,128,128]{3,2,1,0:T(8,128)(2,1)S(1)} %join.10.refs_0_), channel_id=1, source_target_pairs={{0,1},{1,0},{2,3},{3,2},{4,5},{5,4},{6,7},{7,6},{8,9},{9,8},{10,11... | collective-permute-start | bytes 786440 | tf_op jit(solution)/shard_map/ppermute | solution.py:302
  22.0 6.4 %collective-permute-start.8 = (bf16[4,2,128,128]{3,2,1,0:T(8,128)(2,1)S(1)}, bf16[4,2,128,128]{3,2,1,0:T(8,128)(2,1)S(1)}, u32[]{:S(2)}, u32[]{:S(2)}) collective-permute-start(bf16[4,2,128,128]{3,2,1,0:T(8,128)(2,1)S(1)} %join.10.refs_0_), channel_id=1, source_target_pairs={{0,4},{4,8},{8,12},{12,14},{14,10},{10,6},{6,2},{2,0},{1,3},{5,1},... | collective-permute-start | bytes 786440 | tf_op jit(solution)/shard_map/ppermute | solution.py:302
  24.9 3.5 %collective-permute-start.14 = (bf16[4,2,128,128]{3,2,1,0:T(8,128)(2,1)S(1)}, bf16[4,2,128,128]{3,2,1,0:T(8,128)(2,1)S(1)}, u32[]{:S(2)}, u32[]{:S(2)}) collective-permute-start(bf16[4,2,128,128]{3,2,1,0:T(8,128)(2,1)S(1)} %join.12.refs_2_), channel_id=1, source_target_pairs={{0,1},{1,0},{2,3},{3,2},{4,5},{5,4},{6,7},{7,6},{8,9},{9,8},{10,11... | collective-permute-start | bytes 786440 | tf_op jit(solution)/shard_map/ppermute | solution.py:302
  28.4 1.5 %collective-permute-start.13 = (bf16[4,2,128,128]{3,2,1,0:T(8,128)(2,1)S(1)}, bf16[4,2,128,128]{3,2,1,0:T(8,128)(2,1)S(1)}, u32[]{:S(2)}, u32[]{:S(2)}) collective-permute-start(bf16[4,2,128,128]{3,2,1,0:T(8,128)(2,1)S(1)} %join.13.refs_1_), channel_id=1, source_target_pairs={{0,1},{1,0},{2,3},{3,2},{4,5},{5,4},{6,7},{7,6},{8,9},{9,8},{10,11... | collective-permute-start | bytes 786440 | tf_op jit(solution)/shard_map/ppermute | solution.py:302

commit v3 on v2

--- a/solution.py
+++ b/solution.py
@@ -11,7 +11,6 @@
 VMEM = pl.BlockSpec(memory_space=pltpu.VMEM)
 ANY = pl.BlockSpec(memory_space=pl.ANY)
 TOKEN = (8, 128)
-GROUP = 2
 PACE = 1150000000
 LIMIT = pltpu.CompilerParams(vmem_limit_bytes=16 << 20)
 
@@ -30,36 +29,39 @@
     return pltpu.with_memory_space_constraint(x, pltpu.HBM)
 
 
-def mask_kernel(length_hbm, blocks_hbm, out_ref, length_ref, blocks_ref, sems):
+def mask_kernel(length_hbm, blocks_hbm, left_hbm, owner_hbm, slot_hbm, out_ref, left_ref, owner_ref, slot_ref, length_ref, blocks_ref, sems):
     sectors, terms, size, _ = blocks_ref.shape
-    lengths = pltpu.make_async_copy(length_hbm, length_ref, sems.at[sectors])
+    pairs = [(length_hbm, length_ref), (left_hbm, left_ref), (owner_hbm, owner_ref), (slot_hbm, slot_ref)]
+    scalars = [pltpu.make_async_copy(source, target, sems.at[sectors + i]) for i, (source, target) in enumerate(pairs)]
     blocks = [pltpu.make_async_copy(blocks_hbm.at[b], blocks_ref.at[b], sems.at[b]) for b in range(sectors)]
-    lengths.start()
-    for copy in blocks:
+    for copy in scalars[:1] + blocks + scalars[1:]:
         copy.start()
-    lengths.wait()
+    scalars[0].wait()
     for b in range(sectors):
         keep = live(size, length_ref[b])
         blocks[b].wait()
         for k in range(terms):
             block = blocks_ref[b, k]
             out_ref[b, k] = jnp.where(keep, block, jnp.zeros_like(block))
-
-
-def mask_right(lengths, blocks):
+    for copy in scalars[1:]:
+        copy.wait()
+
+
+def mask_right(lengths, blocks, *scalars):
     return pl.pallas_call(
         mask_kernel,
-        in_specs=[ANY, ANY],
-        out_specs=VMEM,
-        out_shape=pltpu.VMEM(blocks.shape, blocks.dtype),
+        in_specs=[ANY] * 5,
+        out_specs=[VMEM, SMEM, SMEM, SMEM],
+        out_shape=[pltpu.VMEM(blocks.shape, blocks.dtype)] + [pltpu.SMEM(x.shape, x.dtype) for x in scalars],
         scratch_shapes=[
             pltpu.SMEM(lengths.shape, jnp.int32),
             pltpu.VMEM(blocks.shape, blocks.dtype),
-            pltpu.SemaphoreType.DMA((blocks.shape[0] + 1,)),
+            pltpu.SemaphoreType.DMA((blocks.shape[0] + 1 + len(scalars),)),
         ],
         compiler_params=pltpu.CompilerParams(vmem_limit_bytes=2 << 20),
+        cost_estimate=pl.CostEstimate(flops=10 * PACE, bytes_accessed=0, transcendentals=0),
         name="mask_right",
-    )(hbm(lengths), hbm(blocks))
+    )(*map(hbm, (lengths, blocks, *scalars)))
 
 
 def join_kernel(block_ref, token_ref, out_ref):
@@ -94,42 +96,20 @@
                         both[k * size:(k + 1) * size, i * size:(i + 1) * size])
 
 
-def opening_kernel(high, cap, slots, origins, length_hbm, owner_hbm, slot_hbm, left_hbm, wave_hbm,
-                   partial_ref, token_ref, work_ref, count_ref, length_ref, left_ref, wave_ref,
-                   owner_ref, slot_ref, place_ref, sems, scalar_sems):
-    sectors, partners = wave_hbm.shape[:2]
-    scalars = [
-        pltpu.make_async_copy(source, target, scalar_sems.at[i])
-        for i, (source, target) in enumerate(((length_hbm, length_ref), (owner_hbm, owner_ref), (slot_hbm, slot_ref)))]
-    arrays = []
-    for g in range(sectors // GROUP):
-        at = pl.ds(g * GROUP, GROUP)
-        arrays.append([
-            pltpu.make_async_copy(left_hbm.at[at], left_ref.at[at], sems.at[0, g]),
-            pltpu.make_async_copy(wave_hbm.at[at], wave_ref.at[at], sems.at[1, g])])
-    for copy in scalars + sum(arrays, []):
-        copy.start()
+def opening_kernel(high, cap, slots, origins, length_ref, owner_ref, slot_ref, left_ref, wave_ref,
+                   partial_ref, token_ref, work_ref, count_ref, place_ref):
+    sectors, partners = wave_ref.shape[:2]
     token_ref[...] = jnp.zeros_like(token_ref)
     for c, origin in enumerate(origins(lax.axis_index("sect"))):
         place_ref[origin] = c
         count_ref[c] = 0
-    for copy in scalars:
-        copy.wait()
     for a in range(sectors):
         for j in range(partners):
             chunk = place_ref[owner_ref[j, a]]
             filled = count_ref[chunk]
             count_ref[chunk] = filled + 1
             work_ref[chunk * cap + filled] = (a * partners + j) * slots + slot_ref[j, a]
-
-    def ready(a):
-        if a % GROUP == 0:
-            for copy in arrays[a // GROUP]:
-                copy.wait()
-
-    multiply_left(0, high, length_ref, left_ref, wave_ref, partial_ref, ready)
-    for a in range(high, sectors):
-        ready(a)
+    multiply_left(0, high, length_ref, left_ref, wave_ref, partial_ref)
 
 
 def opening(high, n, cap, slots, origins, lengths, owner, slot, left, wave):
@@ -137,28 +117,19 @@
     terms = left.shape[1]
     return pl.pallas_call(
         functools.partial(opening_kernel, high, cap, slots, origins),
-        in_specs=[ANY] * 5,
-        out_specs=[VMEM, VMEM, SMEM, SMEM, SMEM, VMEM, VMEM],
+        in_specs=[SMEM] * 3 + [VMEM] * 2,
+        out_specs=[VMEM, VMEM, SMEM, SMEM],
         out_shape=[
             pltpu.VMEM((sectors * partners, size, terms * size), wave.dtype),
             pltpu.VMEM(TOKEN, jnp.float32),
             pltpu.SMEM((n * cap,), jnp.int32),
             pltpu.SMEM((n,), jnp.int32),
-            pltpu.SMEM(lengths.shape, jnp.int32),
-            pltpu.VMEM(left.shape, left.dtype),
-            pltpu.VMEM(wave.shape, wave.dtype),
         ],
-        scratch_shapes=[
-            pltpu.SMEM(owner.shape, jnp.int32),
-            pltpu.SMEM(slot.shape, jnp.int32),
-            pltpu.SMEM((n,), jnp.int32),
-            pltpu.SemaphoreType.DMA((2, sectors // GROUP)),
-            pltpu.SemaphoreType.DMA((3,)),
-        ],
+        scratch_shapes=[pltpu.SMEM((n,), jnp.int32)],
         compiler_params=LIMIT,
         cost_estimate=pl.CostEstimate(flops=PACE, bytes_accessed=0, transcendentals=0),
         name="opening",
-    )(*map(hbm, (lengths, owner, slot, left, wave)))
+    )(lengths, owner, slot, left, wave)
 
 
 def partial_kernel(low, high, length_ref, left_ref, wave_ref, _, partial_ref, token_ref):
@@ -176,7 +147,7 @@
         compiler_params=LIMIT,
         cost_estimate=pl.CostEstimate(flops=PACE, bytes_accessed=0, transcendentals=0),
         name="partials",
-    )(lengths, vmem(left), vmem(wave), vmem(before))
+    )(lengths, left, wave, vmem(before))
 
 
 def product_kernel(first, cap, exact, chunks, flush, given, marked, work_ref, count_ref, partial_ref, *refs):
@@ -301,7 +272,8 @@
     def send(block, perm):
         return lax.ppermute(block, "sect", perm)
 
-    first = mask_right(right_length, right_environment)
+    first, lengths, owner, slot = mask_right(
+        right_length, right_environment, left_length, right_owner.T, right_slot.T)
     held = {(0, 0, 0): first, (1, 0, 0): send(first, onward)}
     held[0, 1, 0] = send(first, across)
     held[1, 1, 0] = send(held[0, 1, 0], onward)
@@ -311,10 +283,10 @@
     windows = [(hop, other) for hop in range(1, hops + 1) for other in (0, 1) if hop < hops or not other]
     for at, (hop, other) in enumerate(windows):
         if not at:
-            part, token, work, count, lengths, left, wave = opening(
-                cuts[0], n, cap, right_environment.shape[0], origins, left_length, right_owner.T, right_slot.T, left_environment, wavefunction)
+            part, token, work, count = opening(
+                cuts[0], n, cap, right_environment.shape[0], origins, lengths, owner, slot, left_environment, wavefunction)
         elif at < len(cuts):
-            part, token = partials(cuts[at - 1], cuts[at], lengths, left, wave, part)
+            part, token = partials(cuts[at - 1], cuts[at], lengths, left_environment, wavefunction, part)
         else:
             upto = 2 * at if at + 1 < len(windows) else 2 * at + 1
             stage, token, out = products(

time: 31 us -> 30.4 us (0.981)
  Pallas kernels: 11.5 us -> 9.54 us
  starting transfers between devices: 13.1 us -> 14.8 us
  waiting for transfers between devices: 6.17 us -> 5.82 us
    pallas_call x1, Pallas kernels: 3.43 us -> 1.31 us  [opening(): pl.pallas_call(functools.partial(opening_kernel, high, cap, slots, origin...]
    ppermute x15, starting transfers between devices: 13.1 us -> 14.8 us  [send(): return lax.ppermute(block, 'sect', perm)]
    ppermute x15, waiting for transfers between devices: 6.17 us -> 5.82 us  [send(): return lax.ppermute(block, 'sect', perm)]
  transfers between devices with their start and end apart: 15 -> 15, of which waited for: 6 -> 7; matrix products, arithmetic and copies ran while one was open for 0% -> 0% of each run, Pallas kernels for 31% -> 25%
where the time goes in v3:
time: 30.4 us; the launch traced here: 30.2 us
  starting transfers between devices  14.8 us (49%)
  Pallas kernels  9.54 us (31%)
  waiting for transfers between devices  5.82 us (19%)
    ppermute x15, starting transfers between devices, send(): return lax.ppermute(block, 'sect', perm)  14.8 us
    ppermute x15, waiting for transfers between devices, send(): return lax.ppermute(block, 'sect', perm)  5.82 us
    pallas_call x6, Pallas kernels, products(): pl.pallas_call(functools.partial(product_kernel, first, cap, exact, chunk...  5.65 us
    pallas_call x2, Pallas kernels, partials(): pl.pallas_call(functools.partial(partial_kernel, low, high), in_specs=[SM...  1.38 us
    pallas_call x1, Pallas kernels, opening(): pl.pallas_call(functools.partial(opening_kernel, high, cap, slots, origin...  1.31 us
    pallas_call x1, Pallas kernels, mask_right(): pl.pallas_call(mask_kernel, in_specs=[ANY] * 5, out_specs=[VMEM, SMEM, SM...  1.2 us
  transfers between devices with their start and end apart: 15, of which 7 were waited for; matrix products, arithmetic and copies ran while one was open for 0% of the time, Pallas kernels for 25%

profile of v3, /device:TPU:0, one launch (start us, length us, event | category | flops | bytes accessed | tf_op | source)
XLA Modules:
  0.0 30.2 jit_solution(9007377622333090120)
XLA Ops:
  0.0 1.2 %mask_right.1 = (bf16[4,2,128,128]{3,2,1,0:T(8,128)(2,1)S(1)}, s32[16]{0:T(128)S(4)}, s32[8,16]{1,0:T(8,128)S(4)}, s32[8,16]{1,0:T(8,128)S(4)}) custom-call(s32[4]{0:T(128)} %length_hbm.1, bf16[4,2,128,128]{3,2,1,0:T(8,128)(2,1)} %blocks_hbm.1, s32[16]{0:T(128)} %left_hbm.1, s32[8,16]{1,0:T(8,128)} %bitcast.3, s32[8,16]{1,0:T(8,128)} %bitcast.4), custom_call_target="tpu_custom_call" | custom-call | flops 11500000256 | tf_op jit(solution)/shard_map/mask_right/pallas_call | solution.py:51
  1.2 0.5 %collective-permute-start.4 = (bf16[4,2,128,128]{3,2,1,0:T(8,128)(2,1)S(1)}, bf16[4,2,128,128]{3,2,1,0:T(8,128)(2,1)S(1)}, u32[]{:S(2)}, u32[]{:S(2)}) collective-permute-start(bf16[4,2,128,128]{3,2,1,0:T(8,128)(2,1)S(1)} %get-tuple-element.37.refs_0_), channel_id=1, source_target_pairs={{0,1},{1,0},{2,3},{3,2},{4,5},{5,4},{6,7},{7,6},{8,9},{9,8},{10,11... | collective-permute-start | bytes 786440 | tf_op jit(solution)/shard_map/ppermute | solution.py:273
  1.7 2.6 %collective-permute-start = (bf16[4,2,128,128]{3,2,1,0:T(8,128)(2,1)S(1)}, bf16[4,2,128,128]{3,2,1,0:T(8,128)(2,1)S(1)}, u32[]{:S(2)}, u32[]{:S(2)}) collective-permute-start(bf16[4,2,128,128]{3,2,1,0:T(8,128)(2,1)S(1)} %get-tuple-element.37.refs_0_), channel_id=1, source_target_pairs={{0,4},{4,8},{8,12},{12,14},{14,10},{10,6},{6,2},{2,0},{1,3},{5,1},... | collective-permute-start | bytes 786440 | tf_op jit(solution)/shard_map/ppermute | solution.py:273
  4.4 1.6 %collective-permute-start.6 = (bf16[4,2,128,128]{3,2,1,0:T(8,128)(2,1)S(1)}, bf16[4,2,128,128]{3,2,1,0:T(8,128)(2,1)S(1)}, u32[]{:S(2)}, u32[]{:S(2)}) collective-permute-start(bf16[4,2,128,128]{3,2,1,0:T(8,128)(2,1)S(1)} %collective-permute-done.4.refs_1_), channel_id=1, source_target_pairs={{0,4},{4,8},{8,12},{12,14},{14,10},{10,6},{6,2},{2,0},{1,3},{5,1},... | collective-permute-start | bytes 786440 | tf_op jit(solution)/shard_map/ppermute | solution.py:273
  6.0 1.3 %opening.1 = (bf16[128,128,256]{2,1,0:T(8,128)(2,1)S(1)}, f32[8,128]{1,0:T(8,128)S(1)}, s32[128]{0:T(128)S(4)}, s32[16]{0:T(128)S(4)}) custom-call(s32[16]{0:T(128)S(4)} %get-tuple-element.29.length_ref, s32[8,16]{1,0:T(8,128)S(4)} %get-tuple-element.30.owner_ref, s32[8,16]{1,0:T(8,128)S(4)} %get-tuple-element.31.slot_ref, ...), custom_call_target="tpu_custom_call" | custom-call | flops 1150000000 | tf_op jit(solution)/shard_map/opening/pallas_call | solution.py:118
  7.3 1.4 %collective-permute-done.block_ref = bf16[4,2,128,128]{3,2,1,0:T(8,128)(2,1)S(1)} collective-permute-done((bf16[4,2,128,128]{3,2,1,0:T(8,128)(2,1)S(1)}, bf16[4,2,128,128]{3,2,1,0:T(8,128)(2,1)S(1)}, u32[]{:S(2)}, u32[]{:S(2)}) %collective-permute-start) | collective-permute-done | bytes 262176 | tf_op jit(solution)/shard_map/ppermute | solution.py:273
  8.6 2.1 %collective-permute-start.1 = (bf16[4,2,128,128]{3,2,1,0:T(8,128)(2,1)S(1)}, bf16[4,2,128,128]{3,2,1,0:T(8,128)(2,1)S(1)}, u32[]{:S(2)}, u32[]{:S(2)}) collective-permute-start(bf16[4,2,128,128]{3,2,1,0:T(8,128)(2,1)S(1)} %join.7.refs_2_), channel_id=1, source_target_pairs={{0,4},{4,8},{8,12},{12,14},{14,10},{10,6},{6,2},{2,0},{1,3},{5,1},... | collective-permute-start | bytes 786440 | tf_op jit(solution)/shard_map/ppermute | solution.py:273
  10.7 0.7 %partials.2 = (bf16[128,128,256]{2,1,0:T(8,128)(2,1)S(1)}, f32[8,128]{1,0:T(8,128)S(1)}) custom-call(s32[16]{0:T(128)S(4)} %get-tuple-element.29.length_ref, bf16[16,2,128,128]{3,2,1,0:T(8,128)(2,1)S(1)} %copy-done.1, bf16[16,8,128,128]{3,2,1,0:T(8,128)(2,1)S(1)} %copy-done, ...), custom_call_target="tpu_custom_call", output_to_operand_aliasing={{0}: (3, {})} | custom-call | flops 1150000000 | tf_op jit(solution)/shard_map/partials/pallas_call | solution.py:141
  11.5 0.5 %collective-permute-start.7 = (bf16[4,2,128,128]{3,2,1,0:T(8,128)(2,1)S(1)}, bf16[4,2,128,128]{3,2,1,0:T(8,128)(2,1)S(1)}, u32[]{:S(2)}, u32[]{:S(2)}) collective-permute-start(bf16[4,2,128,128]{3,2,1,0:T(8,128)(2,1)S(1)} %join.9.refs_4_), channel_id=1, source_target_pairs={{0,1},{1,0},{2,3},{3,2},{4,5},{5,4},{6,7},{7,6},{8,9},{9,8},{10,11... | collective-permute-start | bytes 786440 | tf_op jit(solution)/shard_map/ppermute | solution.py:273
  12.0 1.6 %collective-permute-start.10 = (bf16[4,2,128,128]{3,2,1,0:T(8,128)(2,1)S(1)}, bf16[4,2,128,128]{3,2,1,0:T(8,128)(2,1)S(1)}, u32[]{:S(2)}, u32[]{:S(2)}) collective-permute-start(bf16[4,2,128,128]{3,2,1,0:T(8,128)(2,1)S(1)} %join.9.refs_4_), channel_id=1, source_target_pairs={{0,4},{4,8},{8,12},{12,14},{14,10},{10,6},{6,2},{2,0},{1,3},{5,1},... | collective-permute-start | bytes 786440 | tf_op jit(solution)/shard_map/ppermute | solution.py:273
  13.6 0.7 %partials.3 = (bf16[128,128,256]{2,1,0:T(8,128)(2,1)S(1)}, f32[8,128]{1,0:T(8,128)S(1)}) custom-call(s32[16]{0:T(128)S(4)} %get-tuple-element.29.length_ref, bf16[16,2,128,128]{3,2,1,0:T(8,128)(2,1)S(1)} %copy-done.1, bf16[16,8,128,128]{3,2,1,0:T(8,128)(2,1)S(1)} %copy-done, ...), custom_call_target="tpu_custom_call", output_to_operand_aliasing={{0}: (3, {})} | custom-call | flops 1150000000 | tf_op jit(solution)/shard_map/partials/pallas_call | solution.py:141
  14.3 0.7 %collective-permute-done.1.block_ref = bf16[4,2,128,128]{3,2,1,0:T(8,128)(2,1)S(1)} collective-permute-done((bf16[4,2,128,128]{3,2,1,0:T(8,128)(2,1)S(1)}, bf16[4,2,128,128]{3,2,1,0:T(8,128)(2,1)S(1)}, u32[]{:S(2)}, u32[]{:S(2)}) %collective-permute-start.1) | collective-permute-done | bytes 262176 | tf_op jit(solution)/shard_map/ppermute | solution.py:273
  15.0 2.1 %collective-permute-start.2 = (bf16[4,2,128,128]{3,2,1,0:T(8,128)(2,1)S(1)}, bf16[4,2,128,128]{3,2,1,0:T(8,128)(2,1)S(1)}, u32[]{:S(2)}, u32[]{:S(2)}) collective-permute-start(bf16[4,2,128,128]{3,2,1,0:T(8,128)(2,1)S(1)} %join.8.refs_0_), channel_id=1, source_target_pairs={{0,4},{4,8},{8,12},{12,14},{14,10},{10,6},{6,2},{2,0},{1,3},{5,1},... | collective-permute-start | bytes 786440 | tf_op jit(solution)/shard_map/ppermute | solution.py:273
  17.1 1.0 %products.6 = (bf16[128,128,128]{2,1,0:T(8,128)(2,1)S(1)}, f32[8,128]{1,0:T(8,128)S(1)}) custom-call(s32[128]{0:T(128)S(4)} %get-tuple-element.32.work_ref, s32[16]{0:T(128)S(4)} %get-tuple-element.33.count_ref, bf16[128,128,256]{2,1,0:T(8,128)(2,1)S(1)} %get-tuple-element.36.partial_ref, bf16[4,2,128,128]{3,2,1,0:T(8,128)(2,1)S(1)} %get-tuple-element.37.refs_0_, ...), custom_call_target="tpu_custom_call" | custom-call | flops 1150000000 | tf_op jit(solution)/shard_map/products/pallas_call | solution.py:224
  18.4 1.6 %collective-permute-start.11 = (bf16[4,2,128,128]{3,2,1,0:T(8,128)(2,1)S(1)}, bf16[4,2,128,128]{3,2,1,0:T(8,128)(2,1)S(1)}, u32[]{:S(2)}, u32[]{:S(2)}) collective-permute-start(bf16[4,2,128,128]{3,2,1,0:T(8,128)(2,1)S(1)} %join.11.refs_0_), channel_id=1, source_target_pairs={{0,4},{4,8},{8,12},{12,14},{14,10},{10,6},{6,2},{2,0},{1,3},{5,1},... | collective-permute-start | bytes 786440 | tf_op jit(solution)/shard_map/ppermute | solution.py:273
  20.0 0.4 %products.7 = (bf16[128,128,128]{2,1,0:T(8,128)(2,1)S(1)}, f32[8,128]{1,0:T(8,128)S(1)}) custom-call(s32[128]{0:T(128)S(4)} %get-tuple-element.32.work_ref, s32[16]{0:T(128)S(4)} %get-tuple-element.33.count_ref, bf16[128,128,256]{2,1,0:T(8,128)(2,1)S(1)} %get-tuple-element.36.partial_ref, ...), custom_call_target="tpu_custom_call", output_to_operand_aliasing={{0}: (5, {})} | custom-call | flops 1150000000 | tf_op jit(solution)/shard_map/products/pallas_call | solution.py:224
  20.4 1.0 %collective-permute-done.2.block_ref = bf16[4,2,128,128]{3,2,1,0:T(8,128)(2,1)S(1)} collective-permute-done((bf16[4,2,128,128]{3,2,1,0:T(8,128)(2,1)S(1)}, bf16[4,2,128,128]{3,2,1,0:T(8,128)(2,1)S(1)}, u32[]{:S(2)}, u32[]{:S(2)}) %collective-permute-start.2) | collective-permute-done | bytes 262176 | tf_op jit(solution)/shard_map/ppermute | solution.py:273
  21.4 2.1 %collective-permute-start.8 = (bf16[4,2,128,128]{3,2,1,0:T(8,128)(2,1)S(1)}, bf16[4,2,128,128]{3,2,1,0:T(8,128)(2,1)S(1)}, u32[]{:S(2)}, u32[]{:S(2)}) collective-permute-start(bf16[4,2,128,128]{3,2,1,0:T(8,128)(2,1)S(1)} %join.10.refs_0_), channel_id=1, source_target_pairs={{0,4},{4,8},{8,12},{12,14},{14,10},{10,6},{6,2},{2,0},{1,3},{5,1},... | collective-permute-start | bytes 786440 | tf_op jit(solution)/shard_map/ppermute | solution.py:273
  23.9 0.8 %collective-permute-done.11.block_ref = bf16[4,2,128,128]{3,2,1,0:T(8,128)(2,1)S(1)} collective-permute-done((bf16[4,2,128,128]{3,2,1,0:T(8,128)(2,1)S(1)}, bf16[4,2,128,128]{3,2,1,0:T(8,128)(2,1)S(1)}, u32[]{:S(2)}, u32[]{:S(2)}) %collective-permute-start.11) | collective-permute-done | bytes 262176 | tf_op jit(solution)/shard_map/ppermute | solution.py:273
  24.8 1.7 %products.9 = (bf16[128,128,128]{2,1,0:T(8,128)(2,1)S(1)}, f32[8,128]{1,0:T(8,128)S(1)}, bf16[128,128,128]{2,1,0:T(8,128)(2,1)}) custom-call(s32[128]{0:T(128)S(4)} %get-tuple-element.32.work_ref, s32[16]{0:T(128)S(4)} %get-tuple-element.33.count_ref, bf16[128,128,256]{2,1,0:T(8,128)(2,1)S(1)} %get-tuple-element.36.partial_ref, ...), custom_call_target="tpu_custom_call", output_to_operand_aliasing={{0}: (6, {})} | custom-call | flops 1150000000 | tf_op jit(solution)/shard_map/products/pallas_call | solution.py:224
  26.5 1.2 %collective-permute-done.8.block_ref = bf16[4,2,128,128]{3,2,1,0:T(8,128)(2,1)S(1)} collective-permute-done((bf16[4,2,128,128]{3,2,1,0:T(8,128)(2,1)S(1)}, bf16[4,2,128,128]{3,2,1,0:T(8,128)(2,1)S(1)}, u32[]{:S(2)}, u32[]{:S(2)}) %collective-permute-start.8) | collective-permute-done | bytes 262176 | tf_op jit(solution)/shard_map/ppermute | solution.py:273
  27.8 1.1 %products.10 = (bf16[128,128,128]{2,1,0:T(8,128)(2,1)S(1)}, bf16[128,128,128]{2,1,0:T(8,128)(2,1)}) custom-call(s32[128]{0:T(128)S(4)} %get-tuple-element.32.work_ref, s32[16]{0:T(128)S(4)} %get-tuple-element.33.count_ref, bf16[128,128,256]{2,1,0:T(8,128)(2,1)S(1)} %get-tuple-element.36.partial_ref, ...), custom_call_target="tpu_custom_call", output_to_operand_aliasing={{0}: (5, {}), {1}: (6, {})} | custom-call | flops 1150000000 | tf_op jit(solution)/shard_map/products/pallas_call | solution.py:224
  28.9 0.4 %collective-permute-done.13.refs_0_ = bf16[4,2,128,128]{3,2,1,0:T(8,128)(2,1)S(1)} collective-permute-done((bf16[4,2,128,128]{3,2,1,0:T(8,128)(2,1)S(1)}, bf16[4,2,128,128]{3,2,1,0:T(8,128)(2,1)S(1)}, u32[]{:S(2)}, u32[]{:S(2)}) %collective-permute-start.13) | collective-permute-done | bytes 262176 | tf_op jit(solution)/shard_map/ppermute | solution.py:273
  29.3 0.9 %products.11 = (bf16[128,128,128]{2,1,0:T(8,128)(2,1)S(1)}, bf16[128,128,128]{2,1,0:T(8,128)(2,1)}) custom-call(s32[128]{0:T(128)S(4)} %get-tuple-element.32.work_ref, s32[16]{0:T(128)S(4)} %get-tuple-element.33.count_ref, bf16[128,128,256]{2,1,0:T(8,128)(2,1)S(1)} %get-tuple-element.36.partial_ref, ...), custom_call_target="tpu_custom_call", output_to_operand_aliasing={{0}: (4, {}), {1}: (5, {})} | custom-call | flops 1150000000 | tf_op jit(solution)/shard_map/products/pallas_call | solution.py:224
  (27 shorter events, 0.8 us)
Async XLA Ops:
  0.0 5.9 %copy-start = (bf16[16,8,128,128]{3,2,1,0:T(8,128)(2,1)S(1)}, bf16[16,8,128,128]{3,2,1,0:T(8,128)(2,1)}, u32[]{:S(2)}) copy-start(bf16[16,8,128,128]{3,2,1,0:T(8,128)(2,1)} %wave_ref.5) | copy-start | bytes 12582916
  0.0 5.9 %copy-start.1 = (bf16[16,2,128,128]{3,2,1,0:T(8,128)(2,1)S(1)}, bf16[16,2,128,128]{3,2,1,0:T(8,128)(2,1)}, u32[]{:S(2)}) copy-start(bf16[16,2,128,128]{3,2,1,0:T(8,128)(2,1)} %left_ref.5) | copy-start | bytes 3145732
  1.2 3.2 %collective-permute-start.4 = (bf16[4,2,128,128]{3,2,1,0:T(8,128)(2,1)S(1)}, bf16[4,2,128,128]{3,2,1,0:T(8,128)(2,1)S(1)}, u32[]{:S(2)}, u32[]{:S(2)}) collective-permute-start(bf16[4,2,128,128]{3,2,1,0:T(8,128)(2,1)S(1)} %get-tuple-element.37.refs_0_), channel_id=1, source_target_pairs={{0,1},{1,0},{2,3},{3,2},{4,5},{5,4},{6,7},{7,6},{8,9},{9,8},{10,11... | collective-permute-start | bytes 786440 | tf_op jit(solution)/shard_map/ppermute | solution.py:273
  1.7 6.9 %collective-permute-start = (bf16[4,2,128,128]{3,2,1,0:T(8,128)(2,1)S(1)}, bf16[4,2,128,128]{3,2,1,0:T(8,128)(2,1)S(1)}, u32[]{:S(2)}, u32[]{:S(2)}) collective-permute-start(bf16[4,2,128,128]{3,2,1,0:T(8,128)(2,1)S(1)} %get-tuple-element.37.refs_0_), channel_id=1, source_target_pairs={{0,4},{4,8},{8,12},{12,14},{14,10},{10,6},{6,2},{2,0},{1,3},{5,1},... | collective-permute-start | bytes 786440 | tf_op jit(solution)/shard_map/ppermute | solution.py:273
  4.4 7.2 %collective-permute-start.6 = (bf16[4,2,128,128]{3,2,1,0:T(8,128)(2,1)S(1)}, bf16[4,2,128,128]{3,2,1,0:T(8,128)(2,1)S(1)}, u32[]{:S(2)}, u32[]{:S(2)}) collective-permute-start(bf16[4,2,128,128]{3,2,1,0:T(8,128)(2,1)S(1)} %collective-permute-done.4.refs_1_), channel_id=1, source_target_pairs={{0,4},{4,8},{8,12},{12,14},{14,10},{10,6},{6,2},{2,0},{1,3},{5,1},... | collective-permute-start | bytes 786440 | tf_op jit(solution)/shard_map/ppermute | solution.py:273
  8.6 6.4 %collective-permute-start.1 = (bf16[4,2,128,128]{3,2,1,0:T(8,128)(2,1)S(1)}, bf16[4,2,128,128]{3,2,1,0:T(8,128)(2,1)S(1)}, u32[]{:S(2)}, u32[]{:S(2)}) collective-permute-start(bf16[4,2,128,128]{3,2,1,0:T(8,128)(2,1)S(1)} %join.7.refs_2_), channel_id=1, source_target_pairs={{0,4},{4,8},{8,12},{12,14},{14,10},{10,6},{6,2},{2,0},{1,3},{5,1},... | collective-permute-start | bytes 786440 | tf_op jit(solution)/shard_map/ppermute | solution.py:273
  11.4 5.7 %collective-permute-start.5 = (bf16[4,2,128,128]{3,2,1,0:T(8,128)(2,1)S(1)}, bf16[4,2,128,128]{3,2,1,0:T(8,128)(2,1)S(1)}, u32[]{:S(2)}, u32[]{:S(2)}) collective-permute-start(bf16[4,2,128,128]{3,2,1,0:T(8,128)(2,1)S(1)} %join.7.refs_2_), channel_id=1, source_target_pairs={{0,1},{1,0},{2,3},{3,2},{4,5},{5,4},{6,7},{7,6},{8,9},{9,8},{10,11... | collective-permute-start | bytes 786440 | tf_op jit(solution)/shard_map/ppermute | solution.py:273
  11.5 5.6 %collective-permute-start.7 = (bf16[4,2,128,128]{3,2,1,0:T(8,128)(2,1)S(1)}, bf16[4,2,128,128]{3,2,1,0:T(8,128)(2,1)S(1)}, u32[]{:S(2)}, u32[]{:S(2)}) collective-permute-start(bf16[4,2,128,128]{3,2,1,0:T(8,128)(2,1)S(1)} %join.9.refs_4_), channel_id=1, source_target_pairs={{0,1},{1,0},{2,3},{3,2},{4,5},{5,4},{6,7},{7,6},{8,9},{9,8},{10,11... | collective-permute-start | bytes 786440 | tf_op jit(solution)/shard_map/ppermute | solution.py:273
  12.0 6.4 %collective-permute-start.10 = (bf16[4,2,128,128]{3,2,1,0:T(8,128)(2,1)S(1)}, bf16[4,2,128,128]{3,2,1,0:T(8,128)(2,1)S(1)}, u32[]{:S(2)}, u32[]{:S(2)}) collective-permute-start(bf16[4,2,128,128]{3,2,1,0:T(8,128)(2,1)S(1)} %join.9.refs_4_), channel_id=1, source_target_pairs={{0,4},{4,8},{8,12},{12,14},{14,10},{10,6},{6,2},{2,0},{1,3},{5,1},... | collective-permute-start | bytes 786440 | tf_op jit(solution)/shard_map/ppermute | solution.py:273
  15.0 5.0 %collective-permute-start.3 = (bf16[4,2,128,128]{3,2,1,0:T(8,128)(2,1)S(1)}, bf16[4,2,128,128]{3,2,1,0:T(8,128)(2,1)S(1)}, u32[]{:S(2)}, u32[]{:S(2)}) collective-permute-start(bf16[4,2,128,128]{3,2,1,0:T(8,128)(2,1)S(1)} %join.8.refs_0_), channel_id=1, source_target_pairs={{0,1},{1,0},{2,3},{3,2},{4,5},{5,4},{6,7},{7,6},{8,9},{9,8},{10,11... | collective-permute-start | bytes 786440 | tf_op jit(solution)/shard_map/ppermute | solution.py:273
  15.0 6.4 %collective-permute-start.2 = (bf16[4,2,128,128]{3,2,1,0:T(8,128)(2,1)S(1)}, bf16[4,2,128,128]{3,2,1,0:T(8,128)(2,1)S(1)}, u32[]{:S(2)}, u32[]{:S(2)}) collective-permute-start(bf16[4,2,128,128]{3,2,1,0:T(8,128)(2,1)S(1)} %join.8.refs_0_), channel_id=1, source_target_pairs={{0,4},{4,8},{8,12},{12,14},{14,10},{10,6},{6,2},{2,0},{1,3},{5,1},... | collective-permute-start | bytes 786440 | tf_op jit(solution)/shard_map/ppermute | solution.py:273
  18.4 5.1 %collective-permute-start.12 = (bf16[4,2,128,128]{3,2,1,0:T(8,128)(2,1)S(1)}, bf16[4,2,128,128]{3,2,1,0:T(8,128)(2,1)S(1)}, u32[]{:S(2)}, u32[]{:S(2)}) collective-permute-start(bf16[4,2,128,128]{3,2,1,0:T(8,128)(2,1)S(1)} %join.11.refs_0_), channel_id=1, source_target_pairs={{0,1},{1,0},{2,3},{3,2},{4,5},{5,4},{6,7},{7,6},{8,9},{9,8},{10,11... | collective-permute-start | bytes 786440 | tf_op jit(solution)/shard_map/ppermute | solution.py:273
  18.4 6.4 %collective-permute-start.11 = (bf16[4,2,128,128]{3,2,1,0:T(8,128)(2,1)S(1)}, bf16[4,2,128,128]{3,2,1,0:T(8,128)(2,1)S(1)}, u32[]{:S(2)}, u32[]{:S(2)}) collective-permute-start(bf16[4,2,128,128]{3,2,1,0:T(8,128)(2,1)S(1)} %join.11.refs_0_), channel_id=1, source_target_pairs={{0,4},{4,8},{8,12},{12,14},{14,10},{10,6},{6,2},{2,0},{1,3},{5,1},... | collective-permute-start | bytes 786440 | tf_op jit(solution)/shard_map/ppermute | solution.py:273
  21.4 3.4 %collective-permute-start.9 = (bf16[4,2,128,128]{3,2,1,0:T(8,128)(2,1)S(1)}, bf16[4,2,128,128]{3,2,1,0:T(8,128)(2,1)S(1)}, u32[]{:S(2)}, u32[]{:S(2)}) collective-permute-start(bf16[4,2,128,128]{3,2,1,0:T(8,128)(2,1)S(1)} %join.10.refs_0_), channel_id=1, source_target_pairs={{0,1},{1,0},{2,3},{3,2},{4,5},{5,4},{6,7},{7,6},{8,9},{9,8},{10,11... | collective-permute-start | bytes 786440 | tf_op jit(solution)/shard_map/ppermute | solution.py:273
  21.4 6.4 %collective-permute-start.8 = (bf16[4,2,128,128]{3,2,1,0:T(8,128)(2,1)S(1)}, bf16[4,2,128,128]{3,2,1,0:T(8,128)(2,1)S(1)}, u32[]{:S(2)}, u32[]{:S(2)}) collective-permute-start(bf16[4,2,128,128]{3,2,1,0:T(8,128)(2,1)S(1)} %join.10.refs_0_), channel_id=1, source_target_pairs={{0,4},{4,8},{8,12},{12,14},{14,10},{10,6},{6,2},{2,0},{1,3},{5,1},... | collective-permute-start | bytes 786440 | tf_op jit(solution)/shard_map/ppermute | solution.py:273
  24.8 3.0 %collective-permute-start.14 = (bf16[4,2,128,128]{3,2,1,0:T(8,128)(2,1)S(1)}, bf16[4,2,128,128]{3,2,1,0:T(8,128)(2,1)S(1)}, u32[]{:S(2)}, u32[]{:S(2)}) collective-permute-start(bf16[4,2,128,128]{3,2,1,0:T(8,128)(2,1)S(1)} %join.12.refs_2_), channel_id=1, source_target_pairs={{0,1},{1,0},{2,3},{3,2},{4,5},{5,4},{6,7},{7,6},{8,9},{9,8},{10,11... | collective-permute-start | bytes 786440 | tf_op jit(solution)/shard_map/ppermute | solution.py:273
  27.8 1.5 %collective-permute-start.13 = (bf16[4,2,128,128]{3,2,1,0:T(8,128)(2,1)S(1)}, bf16[4,2,128,128]{3,2,1,0:T(8,128)(2,1)S(1)}, u32[]{:S(2)}, u32[]{:S(2)}) collective-permute-start(bf16[4,2,128,128]{3,2,1,0:T(8,128)(2,1)S(1)} %join.13.refs_1_), channel_id=1, source_target_pairs={{0,1},{1,0},{2,3},{3,2},{4,5},{5,4},{6,7},{7,6},{8,9},{9,8},{10,11... | collective-permute-start | bytes 786440 | tf_op jit(solution)/shard_map/ppermute | solution.py:273

commit v4 on v3

--- a/solution.py
+++ b/solution.py
@@ -12,6 +12,8 @@
 ANY = pl.BlockSpec(memory_space=pl.ANY)
 TOKEN = (8, 128)
 PACE = 1150000000
+PACK = PACE
+SMALL = pltpu.CompilerParams(vmem_limit_bytes=2 << 20)
 LIMIT = pltpu.CompilerParams(vmem_limit_bytes=16 << 20)
 
 
@@ -58,26 +60,48 @@
             pltpu.VMEM(blocks.shape, blocks.dtype),
             pltpu.SemaphoreType.DMA((blocks.shape[0] + 1 + len(scalars),)),
         ],
-        compiler_params=pltpu.CompilerParams(vmem_limit_bytes=2 << 20),
-        cost_estimate=pl.CostEstimate(flops=10 * PACE, bytes_accessed=0, transcendentals=0),
+        compiler_params=SMALL,
+        cost_estimate=pl.CostEstimate(flops=11500000000, bytes_accessed=0, transcendentals=0),
         name="mask_right",
     )(*map(hbm, (lengths, blocks, *scalars)))
 
 
-def join_kernel(block_ref, token_ref, out_ref):
-    del block_ref, token_ref, out_ref
-
-
-def join(block, token):
+def join_kernel(block_ref, *refs):
+    del block_ref, refs
+
+
+def join(block, *tokens, cost=0):
     return pl.pallas_call(
         join_kernel,
-        in_specs=[VMEM, VMEM],
+        in_specs=[VMEM] * (1 + len(tokens)),
         out_specs=VMEM,
         out_shape=pltpu.VMEM(block.shape, block.dtype),
         input_output_aliases={0: 0},
-        compiler_params=pltpu.CompilerParams(vmem_limit_bytes=1 << 20),
+        compiler_params=SMALL,
+        cost_estimate=pl.CostEstimate(flops=cost, bytes_accessed=0, transcendentals=0),
         name="join",
-    )(vmem(block), vmem(token))
+    )(vmem(block), *map(vmem, tokens))
+
+
+def pack_kernel(*refs):
+    *block_refs, out_ref, token_ref = refs
+    token_ref[...] = jnp.zeros_like(token_ref)
+    for i, block_ref in enumerate(block_refs):
+        out_ref[i] = block_ref[...]
+
+
+def pack(*blocks):
+    return pl.pallas_call(
+        pack_kernel,
+        in_specs=[VMEM] * len(blocks),
+        out_specs=[VMEM, VMEM],
+        out_shape=[
+            pltpu.VMEM((len(blocks), *blocks[0].shape), blocks[0].dtype),
+            pltpu.VMEM(TOKEN, jnp.float32)],
+        compiler_params=SMALL,
+        cost_estimate=pl.CostEstimate(flops=PACK, bytes_accessed=0, transcendentals=0),
+        name="pack",
+    )(*map(vmem, blocks))
 
 
 def multiply_left(low, high, length_ref, left_ref, wave_ref, partial_ref, ready=lambda a: None):
@@ -150,8 +174,10 @@
     )(lengths, left, wave, vmem(before))
 
 
-def product_kernel(first, cap, exact, chunks, flush, given, marked, work_ref, count_ref, partial_ref, *refs):
-    right_refs, refs = refs[:chunks], refs[chunks:]
+def product_kernel(first, cap, exact, places, flush, given, marked, work_ref, count_ref, partial_ref, *refs):
+    chunks = len(places)
+    right_refs = [ref if at is None else ref.at[at] for ref, at in zip(refs, places)]
+    refs = refs[chunks:]
     refs = refs[given:]
     stage, refs = refs[0], refs[1:]
     slots, terms = right_refs[0].shape[:2]
@@ -205,6 +231,7 @@
 
 def products(first, cap, exact, flush, marked, work, count, partial_value, rights, stage, out):
     blocks, size, _ = partial_value.shape
+    rights, places = zip(*rights)
     chunks = len(rights)
     operands = [vmem(stage)] if stage is not None else []
     specs = [VMEM] * len(operands)
@@ -222,7 +249,7 @@
             operands.append(out)
             specs.append(ANY)
     result = pl.pallas_call(
-        functools.partial(product_kernel, first, cap, exact, chunks, flush, len(operands), marked),
+        functools.partial(product_kernel, first, cap, exact, places, flush, len(operands), marked),
         in_specs=[SMEM, SMEM, VMEM] + [VMEM] * chunks + specs,
         out_specs=out_specs,
         out_shape=out_shape,
@@ -254,10 +281,9 @@
     across = [(d, d ^ 1) for d in range(n)]
 
     plan = [(0, 0, 0), (0, 1, 0)]
-    for hop in range(1, hops + 1):
-        plan += [(hop, 0, 0), (hop, 0, 1)]
-        if hop < hops:
-            plan += [(hop, 1, 0), (hop, 1, 1)]
+    for hop in range(1, hops):
+        plan += [(hop, 0, 0), (hop, 1, 0), (hop, 0, 1), (hop, 1, 1)]
+    plan += [(hops, 0, 0), (hops, 0, 1)]
 
     def origins(device):
         core, chip = lax.rem(device, 2), lax.div(device, 2)
@@ -274,12 +300,18 @@
 
     first, lengths, owner, slot = mask_right(
         right_length, right_environment, left_length, right_owner.T, right_slot.T)
+    first = join(first, cost=11500000000)
     held = {(0, 0, 0): first, (1, 0, 0): send(first, onward)}
     held[0, 1, 0] = send(first, across)
     held[1, 1, 0] = send(held[0, 1, 0], onward)
+    within = {}
     part = work = count = stage = out = None
     cuts = [sectors // 2, 3 * sectors // 4, sectors]
-    done = 0
+    done, packs = 0, []
+
+    def chunks(low, high):
+        return [(held[p], within.get(p)) for p in plan[low:high]]
+
     windows = [(hop, other) for hop in range(1, hops + 1) for other in (0, 1) if hop < hops or not other]
     for at, (hop, other) in enumerate(windows):
         if not at:
@@ -288,19 +320,25 @@
         elif at < len(cuts):
             part, token = partials(cuts[at - 1], cuts[at], lengths, left_environment, wavefunction, part)
         else:
-            upto = 2 * at if at + 1 < len(windows) else 2 * at + 1
+            upto = 2 * at - 2 * (at + 1 < len(windows))
             stage, token, out = products(
                 done, cap, exact, 0 if at + 1 == len(windows) else None, True, work, count, part,
-                [held[p] for p in plan[done:upto]], stage, out)
+                chunks(done, upto), stage, out)
             done = upto
-        here = held[hop, other, 0] = join(held[hop, other, 0], token)
+        here = held[hop, other, 0] = join(held[hop, other, 0], token, *packs, cost=PACE)
+        packs = []
         if hop + 1 + other <= hops:
             held[hop + 1, other, 0] = send(here, onward)
-        held[hop, other, 1] = send(here, across)
+        if other:
+            both, mark = pack(held[hop, 0, 0], here)
+            packs = [mark]
+            held[hop, 0, 1] = held[hop, 1, 1] = send(both, across)
+            within[hop, 0, 1], within[hop, 1, 1] = 0, 1
+    held[hops, 0, 1] = send(held[hops, 0, 0], across)
     flushed = done
     for upto in (n - 1, n):
         stage, token, out = products(
-            done, cap, exact, flushed, False, work, count, part, [held[p] for p in plan[done:upto]], stage, out)
+            done, cap, exact, flushed, False, work, count, part, chunks(done, upto), stage, out)
         done = flushed = upto
     return out.reshape(wavefunction.shape)
 

time: 30.4 us -> 30.3 us (level)
  waiting for transfers between devices: 5.82 us -> 5.18 us
  starting transfers between devices: 14.8 us -> 15.4 us
    ppermute x15 -> x12, starting transfers between devices: 14.8 us -> 15.4 us  [send(): return lax.ppermute(block, 'sect', perm)]
    ppermute x15 -> x12, waiting for transfers between devices: 5.82 us -> 5.18 us  [send(): return lax.ppermute(block, 'sect', perm)]
    pallas_call x13 -> x17, Pallas kernels: 5.66 us -> 5.58 us  [the longest x6 5.47 us: products(): pl.pallas_call(functools.partial(product_kernel, first, cap, exact, place...]
  transfers between devices with their start and end apart: 15 -> 12, of which waited for: 7 -> 7; matrix products, arithmetic and copies ran while one was open for 0% -> 0% of each run, Pallas kernels for 25% -> 24%
where the time goes in v4:
time: 30.3 us; the launch traced here: 30.1 us
  starting transfers between devices  15.4 us (51%)
  Pallas kernels  9.33 us (31%)
  waiting for transfers between devices  5.18 us (17%)
    ppermute x12, starting transfers between devices, send(): return lax.ppermute(block, 'sect', perm)  15.4 us
    pallas_call x6, Pallas kernels, products(): pl.pallas_call(functools.partial(product_kernel, first, cap, exact, place...  5.47 us
    ppermute x12, waiting for transfers between devices, send(): return lax.ppermute(block, 'sect', perm)  5.18 us
    pallas_call x2, Pallas kernels, partials(): pl.pallas_call(functools.partial(partial_kernel, low, high), in_specs=[SM...  1.39 us
    pallas_call x1, Pallas kernels, opening(): pl.pallas_call(functools.partial(opening_kernel, high, cap, slots, origin...  1.31 us
    pallas_call x1, Pallas kernels, mask_right(): pl.pallas_call(mask_kernel, in_specs=[ANY] * 5, out_specs=[VMEM, SMEM, SM...  1.05 us
  transfers between devices with their start and end apart: 12, of which 7 were waited for; matrix products, arithmetic and copies ran while one was open for 0% of the time, Pallas kernels for 24%

profile of v4, /device:TPU:0, one launch (start us, length us, event | category | flops | bytes accessed | tf_op | source)
XLA Modules:
  0.0 30.1 jit_solution(17358502700366878897)
XLA Ops:
  0.0 1.0 %mask_right.1 = (bf16[4,2,128,128]{3,2,1,0:T(8,128)(2,1)S(1)}, s32[16]{0:T(128)S(4)}, s32[8,16]{1,0:T(8,128)S(4)}, s32[8,16]{1,0:T(8,128)S(4)}) custom-call(s32[4]{0:T(128)} %length_hbm.1, bf16[4,2,128,128]{3,2,1,0:T(8,128)(2,1)} %blocks_hbm.1, s32[16]{0:T(128)} %left_hbm.1, s32[8,16]{1,0:T(8,128)} %bitcast.3, s32[8,16]{1,0:T(8,128)} %bitcast.4), custom_call_target="tpu_custom_call" | custom-call | flops 11500000256 | tf_op jit(solution)/shard_map/mask_right/pallas_call | solution.py:53
  1.1 0.5 %collective-permute-start.2 = (bf16[4,2,128,128]{3,2,1,0:T(8,128)(2,1)S(1)}, bf16[4,2,128,128]{3,2,1,0:T(8,128)(2,1)S(1)}, u32[]{:S(2)}, u32[]{:S(2)}) collective-permute-start(bf16[4,2,128,128]{3,2,1,0:T(8,128)(2,1)S(1)} %join.8.refs_0_), channel_id=1, source_target_pairs={{0,1},{1,0},{2,3},{3,2},{4,5},{5,4},{6,7},{7,6},{8,9},{9,8},{10,11... | collective-permute-start | bytes 786440 | tf_op jit(solution)/shard_map/ppermute | solution.py:299
  1.6 2.6 %collective-permute-start = (bf16[4,2,128,128]{3,2,1,0:T(8,128)(2,1)S(1)}, bf16[4,2,128,128]{3,2,1,0:T(8,128)(2,1)S(1)}, u32[]{:S(2)}, u32[]{:S(2)}) collective-permute-start(bf16[4,2,128,128]{3,2,1,0:T(8,128)(2,1)S(1)} %join.8.refs_0_), channel_id=1, source_target_pairs={{0,4},{4,8},{8,12},{12,14},{14,10},{10,6},{6,2},{2,0},{1,3},{5,1},... | collective-permute-start | bytes 786440 | tf_op jit(solution)/shard_map/ppermute | solution.py:299
  4.2 1.6 %collective-permute-start.3 = (bf16[4,2,128,128]{3,2,1,0:T(8,128)(2,1)S(1)}, bf16[4,2,128,128]{3,2,1,0:T(8,128)(2,1)S(1)}, u32[]{:S(2)}, u32[]{:S(2)}) collective-permute-start(bf16[4,2,128,128]{3,2,1,0:T(8,128)(2,1)S(1)} %collective-permute-done.2.refs_1_), channel_id=1, source_target_pairs={{0,4},{4,8},{8,12},{12,14},{14,10},{10,6},{6,2},{2,0},{1,3},{5,1},... | collective-permute-start | bytes 786440 | tf_op jit(solution)/shard_map/ppermute | solution.py:299
  5.8 1.3 %opening.1 = (bf16[128,128,256]{2,1,0:T(8,128)(2,1)S(1)}, f32[8,128]{1,0:T(8,128)S(1)}, s32[128]{0:T(128)S(4)}, s32[16]{0:T(128)S(4)}) custom-call(s32[16]{0:T(128)S(4)} %get-tuple-element.35.length_ref, s32[8,16]{1,0:T(8,128)S(4)} %get-tuple-element.36.owner_ref, s32[8,16]{1,0:T(8,128)S(4)} %get-tuple-element.37.slot_ref, ...), custom_call_target="tpu_custom_call" | custom-call | flops 1150000000 | tf_op jit(solution)/shard_map/opening/pallas_call | solution.py:142
  7.1 0.7 %partials.2 = (bf16[128,128,256]{2,1,0:T(8,128)(2,1)S(1)}, f32[8,128]{1,0:T(8,128)S(1)}) custom-call(s32[16]{0:T(128)S(4)} %get-tuple-element.35.length_ref, bf16[16,2,128,128]{3,2,1,0:T(8,128)(2,1)S(1)} %copy-done.1, bf16[16,8,128,128]{3,2,1,0:T(8,128)(2,1)S(1)} %copy-done, ...), custom_call_target="tpu_custom_call", output_to_operand_aliasing={{0}: (3, {})} | custom-call | flops 1150000000 | tf_op jit(solution)/shard_map/partials/pallas_call | solution.py:165
  7.8 0.7 %collective-permute-done.block_ref = bf16[4,2,128,128]{3,2,1,0:T(8,128)(2,1)S(1)} collective-permute-done((bf16[4,2,128,128]{3,2,1,0:T(8,128)(2,1)S(1)}, bf16[4,2,128,128]{3,2,1,0:T(8,128)(2,1)S(1)}, u32[]{:S(2)}, u32[]{:S(2)}) %collective-permute-start) | collective-permute-done | bytes 262176 | tf_op jit(solution)/shard_map/ppermute | solution.py:299
  8.5 2.1 %collective-permute-start.1 = (bf16[4,2,128,128]{3,2,1,0:T(8,128)(2,1)S(1)}, bf16[4,2,128,128]{3,2,1,0:T(8,128)(2,1)S(1)}, u32[]{:S(2)}, u32[]{:S(2)}) collective-permute-start(bf16[4,2,128,128]{3,2,1,0:T(8,128)(2,1)S(1)} %join.9.refs_0_.refs_2_), channel_id=1, source_target_pairs={{0,4},{4,8},{8,12},{12,14},{14,10},{10,6},{6,2},{2,0},{1,3},{5,1},... | collective-permute-start | bytes 786440 | tf_op jit(solution)/shard_map/ppermute | solution.py:299
  10.6 0.7 %collective-permute-done.3.block_ref = bf16[4,2,128,128]{3,2,1,0:T(8,128)(2,1)S(1)} collective-permute-done((bf16[4,2,128,128]{3,2,1,0:T(8,128)(2,1)S(1)}, bf16[4,2,128,128]{3,2,1,0:T(8,128)(2,1)S(1)}, u32[]{:S(2)}, u32[]{:S(2)}) %collective-permute-start.3) | collective-permute-done | bytes 262176 | tf_op jit(solution)/shard_map/ppermute | solution.py:299
  11.3 2.1 %collective-permute-start.6 = (bf16[4,2,128,128]{3,2,1,0:T(8,128)(2,1)S(1)}, bf16[4,2,128,128]{3,2,1,0:T(8,128)(2,1)S(1)}, u32[]{:S(2)}, u32[]{:S(2)}) collective-permute-start(bf16[4,2,128,128]{3,2,1,0:T(8,128)(2,1)S(1)} %join.10.refs_1_.refs_3_), channel_id=1, source_target_pairs={{0,4},{4,8},{8,12},{12,14},{14,10},{10,6},{6,2},{2,0},{1,3},{5,1},... | collective-permute-start | bytes 786440 | tf_op jit(solution)/shard_map/ppermute | solution.py:299
  13.5 0.7 %partials.3 = (bf16[128,128,256]{2,1,0:T(8,128)(2,1)S(1)}, f32[8,128]{1,0:T(8,128)S(1)}) custom-call(s32[16]{0:T(128)S(4)} %get-tuple-element.35.length_ref, bf16[16,2,128,128]{3,2,1,0:T(8,128)(2,1)S(1)} %copy-done.1, bf16[16,8,128,128]{3,2,1,0:T(8,128)(2,1)S(1)} %copy-done, ...), custom_call_target="tpu_custom_call", output_to_operand_aliasing={{0}: (3, {})} | custom-call | flops 1150000000 | tf_op jit(solution)/shard_map/partials/pallas_call | solution.py:165
  14.2 0.6 %collective-permute-done.1.block_ref = bf16[4,2,128,128]{3,2,1,0:T(8,128)(2,1)S(1)} collective-permute-done((bf16[4,2,128,128]{3,2,1,0:T(8,128)(2,1)S(1)}, bf16[4,2,128,128]{3,2,1,0:T(8,128)(2,1)S(1)}, u32[]{:S(2)}, u32[]{:S(2)}) %collective-permute-start.1) | collective-permute-done | bytes 262176 | tf_op jit(solution)/shard_map/ppermute | solution.py:299
  14.9 2.1 %collective-permute-start.4 = (bf16[4,2,128,128]{3,2,1,0:T(8,128)(2,1)S(1)}, bf16[4,2,128,128]{3,2,1,0:T(8,128)(2,1)S(1)}, u32[]{:S(2)}, u32[]{:S(2)}) collective-permute-start(bf16[4,2,128,128]{3,2,1,0:T(8,128)(2,1)S(1)} %join.11.refs_0_), channel_id=1, source_target_pairs={{0,4},{4,8},{8,12},{12,14},{14,10},{10,6},{6,2},{2,0},{1,3},{5,1},... | collective-permute-start | bytes 786440 | tf_op jit(solution)/shard_map/ppermute | solution.py:299
  17.0 0.7 %products.6 = (bf16[128,128,128]{2,1,0:T(8,128)(2,1)S(1)}, f32[8,128]{1,0:T(8,128)S(1)}) custom-call(s32[128]{0:T(128)S(4)} %get-tuple-element.38.work_ref, s32[16]{0:T(128)S(4)} %get-tuple-element.39.count_ref, bf16[128,128,256]{2,1,0:T(8,128)(2,1)S(1)} %get-tuple-element.42.partial_ref, bf16[4,2,128,128]{3,2,1,0:T(8,128)(2,1)S(1)} %join.8.refs_0_, ...), custom_call_target="tpu_custom_call" | custom-call | flops 1150000000 | tf_op jit(solution)/shard_map/products/pallas_call | solution.py:251
  17.7 2.1 %collective-permute-start.9 = (bf16[4,2,128,128]{3,2,1,0:T(8,128)(2,1)S(1)}, bf16[4,2,128,128]{3,2,1,0:T(8,128)(2,1)S(1)}, u32[]{:S(2)}, u32[]{:S(2)}) collective-permute-start(bf16[4,2,128,128]{3,2,1,0:T(8,128)(2,1)S(1)} %join.12.refs_1_), channel_id=1, source_target_pairs={{0,4},{4,8},{8,12},{12,14},{14,10},{10,6},{6,2},{2,0},{1,3},{5,1},... | collective-permute-start | bytes 786440 | tf_op jit(solution)/shard_map/ppermute | solution.py:299
  19.9 0.5 %products.7 = (bf16[128,128,128]{2,1,0:T(8,128)(2,1)S(1)}, f32[8,128]{1,0:T(8,128)S(1)}) custom-call(s32[128]{0:T(128)S(4)} %get-tuple-element.38.work_ref, s32[16]{0:T(128)S(4)} %get-tuple-element.39.count_ref, bf16[128,128,256]{2,1,0:T(8,128)(2,1)S(1)} %get-tuple-element.42.partial_ref, ...), custom_call_target="tpu_custom_call", output_to_operand_aliasing={{0}: (5, {})} | custom-call | flops 1150000000 | tf_op jit(solution)/shard_map/products/pallas_call | solution.py:251
  20.4 0.9 %collective-permute-done.4.block_ref = bf16[4,2,128,128]{3,2,1,0:T(8,128)(2,1)S(1)} collective-permute-done((bf16[4,2,128,128]{3,2,1,0:T(8,128)(2,1)S(1)}, bf16[4,2,128,128]{3,2,1,0:T(8,128)(2,1)S(1)}, u32[]{:S(2)}, u32[]{:S(2)}) %collective-permute-start.4) | collective-permute-done | bytes 262176 | tf_op jit(solution)/shard_map/ppermute | solution.py:299
  21.3 2.1 %collective-permute-start.7 = (bf16[4,2,128,128]{3,2,1,0:T(8,128)(2,1)S(1)}, bf16[4,2,128,128]{3,2,1,0:T(8,128)(2,1)S(1)}, u32[]{:S(2)}, u32[]{:S(2)}) collective-permute-start(bf16[4,2,128,128]{3,2,1,0:T(8,128)(2,1)S(1)} %join.13.refs_2_.refs_0_), channel_id=1, source_target_pairs={{0,4},{4,8},{8,12},{12,14},{14,10},{10,6},{6,2},{2,0},{1,3},{5,1},... | collective-permute-start | bytes 786440 | tf_op jit(solution)/shard_map/ppermute | solution.py:299
  23.4 0.4 %products.8 = (bf16[128,128,128]{2,1,0:T(8,128)(2,1)S(1)}, f32[8,128]{1,0:T(8,128)S(1)}) custom-call(s32[128]{0:T(128)S(4)} %get-tuple-element.38.work_ref, s32[16]{0:T(128)S(4)} %get-tuple-element.39.count_ref, bf16[128,128,256]{2,1,0:T(8,128)(2,1)S(1)} %get-tuple-element.42.partial_ref, ...), custom_call_target="tpu_custom_call", output_to_operand_aliasing={{0}: (5, {})} | custom-call | flops 1150000000 | tf_op jit(solution)/shard_map/products/pallas_call | solution.py:251
  23.8 0.4 %collective-permute-done.9.block_ref = bf16[4,2,128,128]{3,2,1,0:T(8,128)(2,1)S(1)} collective-permute-done((bf16[4,2,128,128]{3,2,1,0:T(8,128)(2,1)S(1)}, bf16[4,2,128,128]{3,2,1,0:T(8,128)(2,1)S(1)}, u32[]{:S(2)}, u32[]{:S(2)}) %collective-permute-start.9) | collective-permute-done | bytes 262176 | tf_op jit(solution)/shard_map/ppermute | solution.py:299
  24.3 1.7 %products.9 = (bf16[128,128,128]{2,1,0:T(8,128)(2,1)S(1)}, f32[8,128]{1,0:T(8,128)S(1)}, bf16[128,128,128]{2,1,0:T(8,128)(2,1)}) custom-call(s32[128]{0:T(128)S(4)} %get-tuple-element.38.work_ref, s32[16]{0:T(128)S(4)} %get-tuple-element.39.count_ref, bf16[128,128,256]{2,1,0:T(8,128)(2,1)S(1)} %get-tuple-element.42.partial_ref, ...), custom_call_target="tpu_custom_call", output_to_operand_aliasing={{0}: (7, {})} | custom-call | flops 1150000000 | tf_op jit(solution)/shard_map/products/pallas_call | solution.py:251
  26.0 1.7 %collective-permute-done.7.block_ref = bf16[4,2,128,128]{3,2,1,0:T(8,128)(2,1)S(1)} collective-permute-done((bf16[4,2,128,128]{3,2,1,0:T(8,128)(2,1)S(1)}, bf16[4,2,128,128]{3,2,1,0:T(8,128)(2,1)S(1)}, u32[]{:S(2)}, u32[]{:S(2)}) %collective-permute-start.7) | collective-permute-done | bytes 262176 | tf_op jit(solution)/shard_map/ppermute | solution.py:299
  27.6 1.2 %products.10 = (bf16[128,128,128]{2,1,0:T(8,128)(2,1)S(1)}, bf16[128,128,128]{2,1,0:T(8,128)(2,1)}) custom-call(s32[128]{0:T(128)S(4)} %get-tuple-element.38.work_ref, s32[16]{0:T(128)S(4)} %get-tuple-element.39.count_ref, bf16[128,128,256]{2,1,0:T(8,128)(2,1)S(1)} %get-tuple-element.42.partial_ref, ...), custom_call_target="tpu_custom_call", output_to_operand_aliasing={{0}: (6, {}), {1}: (7, {})} | custom-call | flops 1150000000 | tf_op jit(solution)/shard_map/products/pallas_call | solution.py:251
  29.2 0.9 %products.11 = (bf16[128,128,128]{2,1,0:T(8,128)(2,1)S(1)}, bf16[128,128,128]{2,1,0:T(8,128)(2,1)}) custom-call(s32[128]{0:T(128)S(4)} %get-tuple-element.38.work_ref, s32[16]{0:T(128)S(4)} %get-tuple-element.39.count_ref, bf16[128,128,256]{2,1,0:T(8,128)(2,1)S(1)} %get-tuple-element.42.partial_ref, ...), custom_call_target="tpu_custom_call", output_to_operand_aliasing={{0}: (4, {}), {1}: (5, {})} | custom-call | flops 1150000000 | tf_op jit(solution)/shard_map/products/pallas_call | solution.py:251
  (25 shorter events, 0.6 us)
Async XLA Ops:
  1.1 4.8 %copy-start = (bf16[16,8,128,128]{3,2,1,0:T(8,128)(2,1)S(1)}, bf16[16,8,128,128]{3,2,1,0:T(8,128)(2,1)}, u32[]{:S(2)}) copy-start(bf16[16,8,128,128]{3,2,1,0:T(8,128)(2,1)} %wave_ref.5) | copy-start | bytes 12582916
  1.1 4.8 %copy-start.1 = (bf16[16,2,128,128]{3,2,1,0:T(8,128)(2,1)S(1)}, bf16[16,2,128,128]{3,2,1,0:T(8,128)(2,1)}, u32[]{:S(2)}) copy-start(bf16[16,2,128,128]{3,2,1,0:T(8,128)(2,1)} %left_ref.5) | copy-start | bytes 3145732
  1.1 3.2 %collective-permute-start.2 = (bf16[4,2,128,128]{3,2,1,0:T(8,128)(2,1)S(1)}, bf16[4,2,128,128]{3,2,1,0:T(8,128)(2,1)S(1)}, u32[]{:S(2)}, u32[]{:S(2)}) collective-permute-start(bf16[4,2,128,128]{3,2,1,0:T(8,128)(2,1)S(1)} %join.8.refs_0_), channel_id=1, source_target_pairs={{0,1},{1,0},{2,3},{3,2},{4,5},{5,4},{6,7},{7,6},{8,9},{9,8},{10,11... | collective-permute-start | bytes 786440 | tf_op jit(solution)/shard_map/ppermute | solution.py:299
  1.6 6.9 %collective-permute-start = (bf16[4,2,128,128]{3,2,1,0:T(8,128)(2,1)S(1)}, bf16[4,2,128,128]{3,2,1,0:T(8,128)(2,1)S(1)}, u32[]{:S(2)}, u32[]{:S(2)}) collective-permute-start(bf16[4,2,128,128]{3,2,1,0:T(8,128)(2,1)S(1)} %join.8.refs_0_), channel_id=1, source_target_pairs={{0,4},{4,8},{8,12},{12,14},{14,10},{10,6},{6,2},{2,0},{1,3},{5,1},... | collective-permute-start | bytes 786440 | tf_op jit(solution)/shard_map/ppermute | solution.py:299
  4.2 7.1 %collective-permute-start.3 = (bf16[4,2,128,128]{3,2,1,0:T(8,128)(2,1)S(1)}, bf16[4,2,128,128]{3,2,1,0:T(8,128)(2,1)S(1)}, u32[]{:S(2)}, u32[]{:S(2)}) collective-permute-start(bf16[4,2,128,128]{3,2,1,0:T(8,128)(2,1)S(1)} %collective-permute-done.2.refs_1_), channel_id=1, source_target_pairs={{0,4},{4,8},{8,12},{12,14},{14,10},{10,6},{6,2},{2,0},{1,3},{5,1},... | collective-permute-start | bytes 786440 | tf_op jit(solution)/shard_map/ppermute | solution.py:299
  8.5 6.4 %collective-permute-start.1 = (bf16[4,2,128,128]{3,2,1,0:T(8,128)(2,1)S(1)}, bf16[4,2,128,128]{3,2,1,0:T(8,128)(2,1)S(1)}, u32[]{:S(2)}, u32[]{:S(2)}) collective-permute-start(bf16[4,2,128,128]{3,2,1,0:T(8,128)(2,1)S(1)} %join.9.refs_0_.refs_2_), channel_id=1, source_target_pairs={{0,4},{4,8},{8,12},{12,14},{14,10},{10,6},{6,2},{2,0},{1,3},{5,1},... | collective-permute-start | bytes 786440 | tf_op jit(solution)/shard_map/ppermute | solution.py:299
  11.3 6.4 %collective-permute-start.6 = (bf16[4,2,128,128]{3,2,1,0:T(8,128)(2,1)S(1)}, bf16[4,2,128,128]{3,2,1,0:T(8,128)(2,1)S(1)}, u32[]{:S(2)}, u32[]{:S(2)}) collective-permute-start(bf16[4,2,128,128]{3,2,1,0:T(8,128)(2,1)S(1)} %join.10.refs_1_.refs_3_), channel_id=1, source_target_pairs={{0,4},{4,8},{8,12},{12,14},{14,10},{10,6},{6,2},{2,0},{1,3},{5,1},... | collective-permute-start | bytes 786440 | tf_op jit(solution)/shard_map/ppermute | solution.py:299
  13.5 6.5 %collective-permute-start.5 = (bf16[2,4,2,128,128]{4,3,2,1,0:T(8,128)(2,1)S(1)}, bf16[2,4,2,128,128]{4,3,2,1,0:T(8,128)(2,1)S(1)}, u32[]{:S(2)}, u32[]{:S(2)}) collective-permute-start(bf16[2,4,2,128,128]{4,3,2,1,0:T(8,128)(2,1)S(1)} %get-tuple-element.48), channel_id=1, source_target_pairs={{0,1},{1,0},{2,3},{3,2},{4,5},{5,4},{6,7},{7,6},{8,9},{9,8},{10,11... | collective-permute-start | bytes 1572872 | tf_op jit(solution)/shard_map/ppermute | solution.py:299
  14.9 6.4 %collective-permute-start.4 = (bf16[4,2,128,128]{3,2,1,0:T(8,128)(2,1)S(1)}, bf16[4,2,128,128]{3,2,1,0:T(8,128)(2,1)S(1)}, u32[]{:S(2)}, u32[]{:S(2)}) collective-permute-start(bf16[4,2,128,128]{3,2,1,0:T(8,128)(2,1)S(1)} %join.11.refs_0_), channel_id=1, source_target_pairs={{0,4},{4,8},{8,12},{12,14},{14,10},{10,6},{6,2},{2,0},{1,3},{5,1},... | collective-permute-start | bytes 786440 | tf_op jit(solution)/shard_map/ppermute | solution.py:299
  17.7 6.4 %collective-permute-start.9 = (bf16[4,2,128,128]{3,2,1,0:T(8,128)(2,1)S(1)}, bf16[4,2,128,128]{3,2,1,0:T(8,128)(2,1)S(1)}, u32[]{:S(2)}, u32[]{:S(2)}) collective-permute-start(bf16[4,2,128,128]{3,2,1,0:T(8,128)(2,1)S(1)} %join.12.refs_1_), channel_id=1, source_target_pairs={{0,4},{4,8},{8,12},{12,14},{14,10},{10,6},{6,2},{2,0},{1,3},{5,1},... | collective-permute-start | bytes 786440 | tf_op jit(solution)/shard_map/ppermute | solution.py:299
  19.8 4.5 %collective-permute-start.8 = (bf16[2,4,2,128,128]{4,3,2,1,0:T(8,128)(2,1)S(1)}, bf16[2,4,2,128,128]{4,3,2,1,0:T(8,128)(2,1)S(1)}, u32[]{:S(2)}, u32[]{:S(2)}) collective-permute-start(bf16[2,4,2,128,128]{4,3,2,1,0:T(8,128)(2,1)S(1)} %get-tuple-element.53), channel_id=1, source_target_pairs={{0,1},{1,0},{2,3},{3,2},{4,5},{5,4},{6,7},{7,6},{8,9},{9,8},{10,11... | collective-permute-start | bytes 1572872 | tf_op jit(solution)/shard_map/ppermute | solution.py:299
  21.3 6.4 %collective-permute-start.7 = (bf16[4,2,128,128]{3,2,1,0:T(8,128)(2,1)S(1)}, bf16[4,2,128,128]{3,2,1,0:T(8,128)(2,1)S(1)}, u32[]{:S(2)}, u32[]{:S(2)}) collective-permute-start(bf16[4,2,128,128]{3,2,1,0:T(8,128)(2,1)S(1)} %join.13.refs_2_.refs_0_), channel_id=1, source_target_pairs={{0,4},{4,8},{8,12},{12,14},{14,10},{10,6},{6,2},{2,0},{1,3},{5,1},... | collective-permute-start | bytes 786440 | tf_op jit(solution)/shard_map/ppermute | solution.py:299
  24.2 3.4 %collective-permute-start.11 = (bf16[2,4,2,128,128]{4,3,2,1,0:T(8,128)(2,1)S(1)}, bf16[2,4,2,128,128]{4,3,2,1,0:T(8,128)(2,1)S(1)}, u32[]{:S(2)}, u32[]{:S(2)}) collective-permute-start(bf16[2,4,2,128,128]{4,3,2,1,0:T(8,128)(2,1)S(1)} %get-tuple-element.59), channel_id=1, source_target_pairs={{0,1},{1,0},{2,3},{3,2},{4,5},{5,4},{6,7},{7,6},{8,9},{9,8},{10,11... | collective-permute-start | bytes 1572872 | tf_op jit(solution)/shard_map/ppermute | solution.py:299
  27.6 1.5 %collective-permute-start.10 = (bf16[4,2,128,128]{3,2,1,0:T(8,128)(2,1)S(1)}, bf16[4,2,128,128]{3,2,1,0:T(8,128)(2,1)S(1)}, u32[]{:S(2)}, u32[]{:S(2)}) collective-permute-start(bf16[4,2,128,128]{3,2,1,0:T(8,128)(2,1)S(1)} %join.15.refs_2_), channel_id=1, source_target_pairs={{0,1},{1,0},{2,3},{3,2},{4,5},{5,4},{6,7},{7,6},{8,9},{9,8},{10,11... | collective-permute-start | bytes 786440 | tf_op jit(solution)/shard_map/ppermute | solution.py:299

commit v5 on v4

--- a/solution.py
+++ b/solution.py
@@ -61,7 +61,7 @@
             pltpu.SemaphoreType.DMA((blocks.shape[0] + 1 + len(scalars),)),
         ],
         compiler_params=SMALL,
-        cost_estimate=pl.CostEstimate(flops=11500000000, bytes_accessed=0, transcendentals=0),
+        cost_estimate=pl.CostEstimate(flops=1150000000, bytes_accessed=0, transcendentals=0),
         name="mask_right",
     )(*map(hbm, (lengths, blocks, *scalars)))
 
@@ -81,6 +81,29 @@
         cost_estimate=pl.CostEstimate(flops=cost, bytes_accessed=0, transcendentals=0),
         name="join",
     )(vmem(block), *map(vmem, tokens))
+
+
+def remask_kernel(block_ref, length_ref, *refs):
+    out_ref = refs[-1]
+    sectors, terms, size, _ = block_ref.shape
+    for b in range(sectors):
+        keep = live(size, jnp.broadcast_to(length_ref[:, b:b + 1], (size, size)))
+        for k in range(terms):
+            block = block_ref[b, k]
+            out_ref[b, k] = jnp.where(keep, block, jnp.zeros_like(block))
+
+
+def remask(block, lengths, *tokens, cost=0):
+    return pl.pallas_call(
+        remask_kernel,
+        in_specs=[VMEM] * (2 + len(tokens)),
+        out_specs=VMEM,
+        out_shape=pltpu.VMEM(block.shape, block.dtype),
+        input_output_aliases={0: 0},
+        compiler_params=SMALL,
+        cost_estimate=pl.CostEstimate(flops=cost, bytes_accessed=0, transcendentals=0),
+        name="remask",
+    )(vmem(block), vmem(lengths), *map(vmem, tokens))
 
 
 def pack_kernel(*refs):
@@ -120,7 +143,7 @@
                         both[k * size:(k + 1) * size, i * size:(i + 1) * size])
 
 
-def opening_kernel(high, cap, slots, origins, length_ref, owner_ref, slot_ref, left_ref, wave_ref,
+def opening_kernel(high, cap, slots, origins, length_ref, owner_ref, slot_ref, left_ref, wave_ref, _,
                    partial_ref, token_ref, work_ref, count_ref, place_ref):
     sectors, partners = wave_ref.shape[:2]
     token_ref[...] = jnp.zeros_like(token_ref)
@@ -136,12 +159,12 @@
     multiply_left(0, high, length_ref, left_ref, wave_ref, partial_ref)
 
 
-def opening(high, n, cap, slots, origins, lengths, owner, slot, left, wave):
+def opening(high, n, cap, slots, origins, lengths, owner, slot, left, wave, after):
     sectors, partners, size, _ = wave.shape
     terms = left.shape[1]
     return pl.pallas_call(
         functools.partial(opening_kernel, high, cap, slots, origins),
-        in_specs=[SMEM] * 3 + [VMEM] * 2,
+        in_specs=[SMEM] * 3 + [VMEM] * 3,
         out_specs=[VMEM, VMEM, SMEM, SMEM],
         out_shape=[
             pltpu.VMEM((sectors * partners, size, terms * size), wave.dtype),
@@ -153,7 +176,7 @@
         compiler_params=LIMIT,
         cost_estimate=pl.CostEstimate(flops=PACE, bytes_accessed=0, transcendentals=0),
         name="opening",
-    )(lengths, owner, slot, left, wave)
+    )(lengths, owner, slot, left, wave, vmem(after))
 
 
 def partial_kernel(low, high, length_ref, left_ref, wave_ref, _, partial_ref, token_ref):
@@ -300,13 +323,15 @@
 
     first, lengths, owner, slot = mask_right(
         right_length, right_environment, left_length, right_owner.T, right_slot.T)
-    first = join(first, cost=11500000000)
-    held = {(0, 0, 0): first, (1, 0, 0): send(first, onward)}
-    held[0, 1, 0] = send(first, across)
+    row = right_length[None]
+    beside, beside_row = send(right_environment, across), send(row, across)
+    came = send(row, onward)
+    held = {(0, 0, 0): first, (1, 0, 0): send(right_environment, onward)}
+    held[0, 1, 0] = remask(beside, beside_row, cost=0)
     held[1, 1, 0] = send(held[0, 1, 0], onward)
     within = {}
     part = work = count = stage = out = None
-    cuts = [sectors // 2, 3 * sectors // 4, sectors]
+    cuts = [sectors // 2, sectors]
     done, packs = 0, []
 
     def chunks(low, high):
@@ -315,17 +340,24 @@
     windows = [(hop, other) for hop in range(1, hops + 1) for other in (0, 1) if hop < hops or not other]
     for at, (hop, other) in enumerate(windows):
         if not at:
+            token = first
+        elif at == 1:
             part, token, work, count = opening(
-                cuts[0], n, cap, right_environment.shape[0], origins, lengths, owner, slot, left_environment, wavefunction)
-        elif at < len(cuts):
-            part, token = partials(cuts[at - 1], cuts[at], lengths, left_environment, wavefunction, part)
+                cuts[0], n, cap, right_environment.shape[0], origins, lengths, owner, slot, left_environment, wavefunction,
+                held[1, 0, 0])
+        elif at == 2:
+            part, token = partials(cuts[0], cuts[1], lengths, left_environment, wavefunction, part)
         else:
             upto = 2 * at - 2 * (at + 1 < len(windows))
             stage, token, out = products(
                 done, cap, exact, 0 if at + 1 == len(windows) else None, True, work, count, part,
                 chunks(done, upto), stage, out)
             done = upto
-        here = held[hop, other, 0] = join(held[hop, other, 0], token, *packs, cost=PACE)
+        if at:
+            here = join(held[hop, other, 0], token, *packs, cost=PACE)
+        else:
+            here = remask(held[hop, other, 0], came, token, cost=PACE)
+        held[hop, other, 0] = here
         packs = []
         if hop + 1 + other <= hops:
             held[hop + 1, other, 0] = send(here, onward)

time: 30.3 us -> 29.7 us (0.980)
  waiting for transfers between devices: 5.18 us -> 4.04 us
  Pallas kernels: 9.33 us -> 9.79 us
    ppermute x12 -> x14, waiting for transfers between devices: 5.18 us -> 4.04 us  [send(): return lax.ppermute(block, 'sect', perm)]
    pallas_call x0 -> x2, Pallas kernels: none -> 0.47 us  [remask(): pl.pallas_call(remask_kernel, in_specs=[VMEM] * (2 + len(tokens)), out_sp...]
    ppermute x12 -> x14, starting transfers between devices: 15.4 us -> 15.6 us  [send(): return lax.ppermute(block, 'sect', perm)]
    pallas_call x2 -> x1, Pallas kernels: 1.39 us -> 1.24 us  [partials(): pl.pallas_call(functools.partial(partial_kernel, low, high), in_specs=[SM...]
  transfers between devices with their start and end apart: 12 -> 14, of which waited for: 7 -> 6; matrix products, arithmetic and copies ran while one was open for 0% -> 0% of each run, Pallas kernels for 24% -> 30%
where the time goes in v5:
time: 29.7 us; the launch traced here: 29.6 us
  starting transfers between devices  15.6 us (53%)
  Pallas kernels  9.79 us (33%)
  waiting for transfers between devices  4.04 us (14%)
    ppermute x14, starting transfers between devices, send(): return lax.ppermute(block, 'sect', perm)  15.6 us
    pallas_call x6, Pallas kernels, products(): pl.pallas_call(functools.partial(product_kernel, first, cap, exact, place...  5.47 us
    ppermute x14, waiting for transfers between devices, send(): return lax.ppermute(block, 'sect', perm)  4.04 us
    pallas_call x1, Pallas kernels, opening(): pl.pallas_call(functools.partial(opening_kernel, high, cap, slots, origin...  1.31 us
    pallas_call x1, Pallas kernels, partials(): pl.pallas_call(functools.partial(partial_kernel, low, high), in_specs=[SM...  1.24 us
    pallas_call x1, Pallas kernels, mask_right(): pl.pallas_call(mask_kernel, in_specs=[ANY] * 5, out_specs=[VMEM, SMEM, SM...  1.2 us
  transfers between devices with their start and end apart: 14, of which 6 were waited for; matrix products, arithmetic and copies ran while one was open for 0% of the time, Pallas kernels for 30%

profile of v5, /device:TPU:0, one launch (start us, length us, event | category | flops | bytes accessed | tf_op | source)
XLA Modules:
  0.0 29.6 jit_solution(13875861667018867196)
XLA Ops:
  0.0 0.5 %collective-permute-start.3 = (bf16[4,2,128,128]{3,2,1,0:T(8,128)(2,1)}, bf16[4,2,128,128]{3,2,1,0:T(8,128)(2,1)S(1)}, u32[]{:S(2)}, u32[]{:S(2)}) collective-permute-start(bf16[4,2,128,128]{3,2,1,0:T(8,128)(2,1)} %blocks_hbm.1), channel_id=1, source_target_pairs={{0,1},{1,0},{2,3},{3,2},{4,5},{5,4},{6,7},{7,6},{8,9},{9,8},{10,11... | collective-permute-start | bytes 786440 | tf_op jit(solution)/shard_map/ppermute | solution.py:322
  0.5 2.6 %collective-permute-start = (bf16[4,2,128,128]{3,2,1,0:T(8,128)(2,1)}, bf16[4,2,128,128]{3,2,1,0:T(8,128)(2,1)S(1)}, u32[]{:S(2)}, u32[]{:S(2)}) collective-permute-start(bf16[4,2,128,128]{3,2,1,0:T(8,128)(2,1)} %blocks_hbm.1), channel_id=1, source_target_pairs={{0,4},{4,8},{8,12},{12,14},{14,10},{10,6},{6,2},{2,0},{1,3},{5,1},... | collective-permute-start | bytes 786440 | tf_op jit(solution)/shard_map/ppermute | solution.py:322
  3.2 1.4 %collective-permute-start.1 = (s32[1,4]{1,0:T(1,128)}, s32[1,4]{1,0:T(1,128)S(1)}, u32[]{:S(2)}, u32[]{:S(2)}) collective-permute-start(s32[1,4]{1,0:T(1,128)} %bitcast.7), channel_id=1, source_target_pairs={{0,4},{4,8},{8,12},{12,14},{14,10},{10,6},{6,2},{2,0},{1,3},{5,1},... | collective-permute-start | bytes 56 | tf_op jit(solution)/shard_map/ppermute | solution.py:322
  4.9 1.6 %collective-permute-start.5 = (bf16[4,2,128,128]{3,2,1,0:T(8,128)(2,1)S(1)}, bf16[4,2,128,128]{3,2,1,0:T(8,128)(2,1)S(1)}, u32[]{:S(2)}, u32[]{:S(2)}) collective-permute-start(bf16[4,2,128,128]{3,2,1,0:T(8,128)(2,1)S(1)} %remask.3.refs_1_), channel_id=1, source_target_pairs={{0,4},{4,8},{8,12},{12,14},{14,10},{10,6},{6,2},{2,0},{1,3},{5,1},... | collective-permute-start | bytes 786440 | tf_op jit(solution)/shard_map/ppermute | solution.py:322
  6.5 1.2 %mask_right.1 = (bf16[4,2,128,128]{3,2,1,0:T(8,128)(2,1)S(1)}, s32[16]{0:T(128)S(4)}, s32[8,16]{1,0:T(8,128)S(4)}, s32[8,16]{1,0:T(8,128)S(4)}) custom-call(s32[4]{0:T(128)} %length_hbm.1, bf16[4,2,128,128]{3,2,1,0:T(8,128)(2,1)} %blocks_hbm.1, s32[16]{0:T(128)} %left_hbm.1, s32[8,16]{1,0:T(8,128)} %bitcast.4, s32[8,16]{1,0:T(8,128)} %bitcast.5), custom_call_target="tpu_custom_call" | custom-call | flops 1150000000 | tf_op jit(solution)/shard_map/mask_right/pallas_call | solution.py:53
  7.7 0.2 remask.2._.refs_0_.refs_2_
  8.0 2.0 %collective-permute-start.2 = (bf16[4,2,128,128]{3,2,1,0:T(8,128)(2,1)S(1)}, bf16[4,2,128,128]{3,2,1,0:T(8,128)(2,1)S(1)}, u32[]{:S(2)}, u32[]{:S(2)}) collective-permute-start(bf16[4,2,128,128]{3,2,1,0:T(8,128)(2,1)S(1)} %remask.2._.refs_0_.refs_2_), channel_id=1, source_target_pairs={{0,4},{4,8},{8,12},{12,14},{14,10},{10,6},{6,2},{2,0},{1,3},{5,1},... | collective-permute-start | bytes 786440 | tf_op jit(solution)/shard_map/ppermute | solution.py:322
  10.0 1.3 %opening.1 = (bf16[128,128,256]{2,1,0:T(8,128)(2,1)S(1)}, f32[8,128]{1,0:T(8,128)S(1)}, s32[128]{0:T(128)S(4)}, s32[16]{0:T(128)S(4)}) custom-call(s32[16]{0:T(128)S(4)} %get-tuple-element.33.length_ref, s32[8,16]{1,0:T(8,128)S(4)} %get-tuple-element.34.owner_ref, s32[8,16]{1,0:T(8,128)S(4)} %get-tuple-element.35.slot_ref, ...), custom_call_target="tpu_custom_call" | custom-call | flops 1150000000 | tf_op jit(solution)/shard_map/opening/pallas_call | solution.py:165
  11.3 1.6 %collective-permute-start.8 = (bf16[4,2,128,128]{3,2,1,0:T(8,128)(2,1)S(1)}, bf16[4,2,128,128]{3,2,1,0:T(8,128)(2,1)S(1)}, u32[]{:S(2)}, u32[]{:S(2)}) collective-permute-start(bf16[4,2,128,128]{3,2,1,0:T(8,128)(2,1)S(1)} %join.6.refs_1_.refs_3_), channel_id=1, source_target_pairs={{0,4},{4,8},{8,12},{12,14},{14,10},{10,6},{6,2},{2,0},{1,3},{5,1},... | collective-permute-start | bytes 786440 | tf_op jit(solution)/shard_map/ppermute | solution.py:322
  13.1 1.2 %partials.1 = (bf16[128,128,256]{2,1,0:T(8,128)(2,1)S(1)}, f32[8,128]{1,0:T(8,128)S(1)}) custom-call(s32[16]{0:T(128)S(4)} %get-tuple-element.33.length_ref, bf16[16,2,128,128]{3,2,1,0:T(8,128)(2,1)S(1)} %copy-done.1, bf16[16,8,128,128]{3,2,1,0:T(8,128)(2,1)S(1)} %copy-done, ...), custom_call_target="tpu_custom_call", output_to_operand_aliasing={{0}: (3, {})} | custom-call | flops 1150000000 | tf_op jit(solution)/shard_map/partials/pallas_call | solution.py:188
  14.4 2.0 %collective-permute-start.6 = (bf16[4,2,128,128]{3,2,1,0:T(8,128)(2,1)S(1)}, bf16[4,2,128,128]{3,2,1,0:T(8,128)(2,1)S(1)}, u32[]{:S(2)}, u32[]{:S(2)}) collective-permute-start(bf16[4,2,128,128]{3,2,1,0:T(8,128)(2,1)S(1)} %join.7.refs_0_), channel_id=1, source_target_pairs={{0,4},{4,8},{8,12},{12,14},{14,10},{10,6},{6,2},{2,0},{1,3},{5,1},... | collective-permute-start | bytes 786440 | tf_op jit(solution)/shard_map/ppermute | solution.py:322
  16.3 0.7 %products.6 = (bf16[128,128,128]{2,1,0:T(8,128)(2,1)S(1)}, f32[8,128]{1,0:T(8,128)S(1)}) custom-call(s32[128]{0:T(128)S(4)} %get-tuple-element.37.work_ref, s32[16]{0:T(128)S(4)} %get-tuple-element.38.count_ref, bf16[128,128,256]{2,1,0:T(8,128)(2,1)S(1)} %get-tuple-element.40.partial_ref, bf16[4,2,128,128]{3,2,1,0:T(8,128)(2,1)S(1)} %get-tuple-element.36.refs_0_, ...), custom_call_target="tpu_custom_call" | custom-call | flops 1150000000 | tf_op jit(solution)/shard_map/products/pallas_call | solution.py:274
  17.1 0.7 %collective-permute-done.8.block_ref = bf16[4,2,128,128]{3,2,1,0:T(8,128)(2,1)S(1)} collective-permute-done((bf16[4,2,128,128]{3,2,1,0:T(8,128)(2,1)S(1)}, bf16[4,2,128,128]{3,2,1,0:T(8,128)(2,1)S(1)}, u32[]{:S(2)}, u32[]{:S(2)}) %collective-permute-start.8) | collective-permute-done | bytes 262176 | tf_op jit(solution)/shard_map/ppermute | solution.py:322
  17.7 1.6 %collective-permute-start.11 = (bf16[4,2,128,128]{3,2,1,0:T(8,128)(2,1)S(1)}, bf16[4,2,128,128]{3,2,1,0:T(8,128)(2,1)S(1)}, u32[]{:S(2)}, u32[]{:S(2)}) collective-permute-start(bf16[4,2,128,128]{3,2,1,0:T(8,128)(2,1)S(1)} %join.8.refs_1_), channel_id=1, source_target_pairs={{0,4},{4,8},{8,12},{12,14},{14,10},{10,6},{6,2},{2,0},{1,3},{5,1},... | collective-permute-start | bytes 786440 | tf_op jit(solution)/shard_map/ppermute | solution.py:322
  19.4 0.5 %products.7 = (bf16[128,128,128]{2,1,0:T(8,128)(2,1)S(1)}, f32[8,128]{1,0:T(8,128)S(1)}) custom-call(s32[128]{0:T(128)S(4)} %get-tuple-element.37.work_ref, s32[16]{0:T(128)S(4)} %get-tuple-element.38.count_ref, bf16[128,128,256]{2,1,0:T(8,128)(2,1)S(1)} %get-tuple-element.40.partial_ref, ...), custom_call_target="tpu_custom_call", output_to_operand_aliasing={{0}: (5, {})} | custom-call | flops 1150000000 | tf_op jit(solution)/shard_map/products/pallas_call | solution.py:274
  19.9 0.8 %collective-permute-done.6.block_ref = bf16[4,2,128,128]{3,2,1,0:T(8,128)(2,1)S(1)} collective-permute-done((bf16[4,2,128,128]{3,2,1,0:T(8,128)(2,1)S(1)}, bf16[4,2,128,128]{3,2,1,0:T(8,128)(2,1)S(1)}, u32[]{:S(2)}, u32[]{:S(2)}) %collective-permute-start.6) | collective-permute-done | bytes 262176 | tf_op jit(solution)/shard_map/ppermute | solution.py:322
  20.8 2.0 %collective-permute-start.9 = (bf16[4,2,128,128]{3,2,1,0:T(8,128)(2,1)S(1)}, bf16[4,2,128,128]{3,2,1,0:T(8,128)(2,1)S(1)}, u32[]{:S(2)}, u32[]{:S(2)}) collective-permute-start(bf16[4,2,128,128]{3,2,1,0:T(8,128)(2,1)S(1)} %join.9.refs_2_.refs_0_), channel_id=1, source_target_pairs={{0,4},{4,8},{8,12},{12,14},{14,10},{10,6},{6,2},{2,0},{1,3},{5,1},... | collective-permute-start | bytes 786440 | tf_op jit(solution)/shard_map/ppermute | solution.py:322
  22.7 0.4 %products.8 = (bf16[128,128,128]{2,1,0:T(8,128)(2,1)S(1)}, f32[8,128]{1,0:T(8,128)S(1)}) custom-call(s32[128]{0:T(128)S(4)} %get-tuple-element.37.work_ref, s32[16]{0:T(128)S(4)} %get-tuple-element.38.count_ref, bf16[128,128,256]{2,1,0:T(8,128)(2,1)S(1)} %get-tuple-element.40.partial_ref, ...), custom_call_target="tpu_custom_call", output_to_operand_aliasing={{0}: (5, {})} | custom-call | flops 1150000000 | tf_op jit(solution)/shard_map/products/pallas_call | solution.py:274
  23.2 0.9 %collective-permute-done.11.block_ref = bf16[4,2,128,128]{3,2,1,0:T(8,128)(2,1)S(1)} collective-permute-done((bf16[4,2,128,128]{3,2,1,0:T(8,128)(2,1)S(1)}, bf16[4,2,128,128]{3,2,1,0:T(8,128)(2,1)S(1)}, u32[]{:S(2)}, u32[]{:S(2)}) %collective-permute-start.11) | collective-permute-done | bytes 262176 | tf_op jit(solution)/shard_map/ppermute | solution.py:322
  24.2 1.7 %products.9 = (bf16[128,128,128]{2,1,0:T(8,128)(2,1)S(1)}, f32[8,128]{1,0:T(8,128)S(1)}, bf16[128,128,128]{2,1,0:T(8,128)(2,1)}) custom-call(s32[128]{0:T(128)S(4)} %get-tuple-element.37.work_ref, s32[16]{0:T(128)S(4)} %get-tuple-element.38.count_ref, bf16[128,128,256]{2,1,0:T(8,128)(2,1)S(1)} %get-tuple-element.40.partial_ref, ...), custom_call_target="tpu_custom_call", output_to_operand_aliasing={{0}: (7, {})} | custom-call | flops 1150000000 | tf_op jit(solution)/shard_map/products/pallas_call | solution.py:274
  25.9 1.2 %collective-permute-done.9.block_ref = bf16[4,2,128,128]{3,2,1,0:T(8,128)(2,1)S(1)} collective-permute-done((bf16[4,2,128,128]{3,2,1,0:T(8,128)(2,1)S(1)}, bf16[4,2,128,128]{3,2,1,0:T(8,128)(2,1)S(1)}, u32[]{:S(2)}, u32[]{:S(2)}) %collective-permute-start.9) | collective-permute-done | bytes 262176 | tf_op jit(solution)/shard_map/ppermute | solution.py:322
  27.1 1.2 %products.10 = (bf16[128,128,128]{2,1,0:T(8,128)(2,1)S(1)}, bf16[128,128,128]{2,1,0:T(8,128)(2,1)}) custom-call(s32[128]{0:T(128)S(4)} %get-tuple-element.37.work_ref, s32[16]{0:T(128)S(4)} %get-tuple-element.38.count_ref, bf16[128,128,256]{2,1,0:T(8,128)(2,1)S(1)} %get-tuple-element.40.partial_ref, ...), custom_call_target="tpu_custom_call", output_to_operand_aliasing={{0}: (6, {}), {1}: (7, {})} | custom-call | flops 1150000000 | tf_op jit(solution)/shard_map/products/pallas_call | solution.py:274
  28.4 0.3 %collective-permute-done.12.refs_0_ = bf16[4,2,128,128]{3,2,1,0:T(8,128)(2,1)S(1)} collective-permute-done((bf16[4,2,128,128]{3,2,1,0:T(8,128)(2,1)S(1)}, bf16[4,2,128,128]{3,2,1,0:T(8,128)(2,1)S(1)}, u32[]{:S(2)}, u32[]{:S(2)}) %collective-permute-start.12) | collective-permute-done | bytes 262176 | tf_op jit(solution)/shard_map/ppermute | solution.py:322
  28.7 0.9 %products.11 = (bf16[128,128,128]{2,1,0:T(8,128)(2,1)S(1)}, bf16[128,128,128]{2,1,0:T(8,128)(2,1)}) custom-call(s32[128]{0:T(128)S(4)} %get-tuple-element.37.work_ref, s32[16]{0:T(128)S(4)} %get-tuple-element.38.count_ref, bf16[128,128,256]{2,1,0:T(8,128)(2,1)S(1)} %get-tuple-element.40.partial_ref, ...), custom_call_target="tpu_custom_call", output_to_operand_aliasing={{0}: (4, {}), {1}: (5, {})} | custom-call | flops 1150000000 | tf_op jit(solution)/shard_map/products/pallas_call | solution.py:274
  (28 shorter events, 0.8 us)
Async XLA Ops:
  0.0 4.6 %collective-permute-start.3 = (bf16[4,2,128,128]{3,2,1,0:T(8,128)(2,1)}, bf16[4,2,128,128]{3,2,1,0:T(8,128)(2,1)S(1)}, u32[]{:S(2)}, u32[]{:S(2)}) collective-permute-start(bf16[4,2,128,128]{3,2,1,0:T(8,128)(2,1)} %blocks_hbm.1), channel_id=1, source_target_pairs={{0,1},{1,0},{2,3},{3,2},{4,5},{5,4},{6,7},{7,6},{8,9},{9,8},{10,11... | collective-permute-start | bytes 786440 | tf_op jit(solution)/shard_map/ppermute | solution.py:322
  0.5 7.3 %collective-permute-start = (bf16[4,2,128,128]{3,2,1,0:T(8,128)(2,1)}, bf16[4,2,128,128]{3,2,1,0:T(8,128)(2,1)S(1)}, u32[]{:S(2)}, u32[]{:S(2)}) collective-permute-start(bf16[4,2,128,128]{3,2,1,0:T(8,128)(2,1)} %blocks_hbm.1), channel_id=1, source_target_pairs={{0,4},{4,8},{8,12},{12,14},{14,10},{10,6},{6,2},{2,0},{1,3},{5,1},... | collective-permute-start | bytes 786440 | tf_op jit(solution)/shard_map/ppermute | solution.py:322
  3.0 1.6 %collective-permute-start.4 = (s32[1,4]{1,0:T(1,128)}, s32[1,4]{1,0:T(1,128)S(1)}, u32[]{:S(2)}, u32[]{:S(2)}) collective-permute-start(s32[1,4]{1,0:T(1,128)} %bitcast.6), channel_id=1, source_target_pairs={{0,1},{1,0},{2,3},{3,2},{4,5},{5,4},{6,7},{7,6},{8,9},{9,8},{10,11... | collective-permute-start | bytes 56 | tf_op jit(solution)/shard_map/ppermute | solution.py:322
  3.2 4.5 %collective-permute-start.1 = (s32[1,4]{1,0:T(1,128)}, s32[1,4]{1,0:T(1,128)S(1)}, u32[]{:S(2)}, u32[]{:S(2)}) collective-permute-start(s32[1,4]{1,0:T(1,128)} %bitcast.7), channel_id=1, source_target_pairs={{0,4},{4,8},{8,12},{12,14},{14,10},{10,6},{6,2},{2,0},{1,3},{5,1},... | collective-permute-start | bytes 56 | tf_op jit(solution)/shard_map/ppermute | solution.py:322
  4.9 6.4 %collective-permute-start.5 = (bf16[4,2,128,128]{3,2,1,0:T(8,128)(2,1)S(1)}, bf16[4,2,128,128]{3,2,1,0:T(8,128)(2,1)S(1)}, u32[]{:S(2)}, u32[]{:S(2)}) collective-permute-start(bf16[4,2,128,128]{3,2,1,0:T(8,128)(2,1)S(1)} %remask.3.refs_1_), channel_id=1, source_target_pairs={{0,4},{4,8},{8,12},{12,14},{14,10},{10,6},{6,2},{2,0},{1,3},{5,1},... | collective-permute-start | bytes 786440 | tf_op jit(solution)/shard_map/ppermute | solution.py:322
  6.5 3.5 %copy-start = (bf16[16,8,128,128]{3,2,1,0:T(8,128)(2,1)S(1)}, bf16[16,8,128,128]{3,2,1,0:T(8,128)(2,1)}, u32[]{:S(2)}) copy-start(bf16[16,8,128,128]{3,2,1,0:T(8,128)(2,1)} %wave_ref.3) | copy-start | bytes 12582916
  6.5 3.5 %copy-start.1 = (bf16[16,2,128,128]{3,2,1,0:T(8,128)(2,1)S(1)}, bf16[16,2,128,128]{3,2,1,0:T(8,128)(2,1)}, u32[]{:S(2)}) copy-start(bf16[16,2,128,128]{3,2,1,0:T(8,128)(2,1)} %left_ref.3) | copy-start | bytes 3145732
  8.0 6.4 %collective-permute-start.2 = (bf16[4,2,128,128]{3,2,1,0:T(8,128)(2,1)S(1)}, bf16[4,2,128,128]{3,2,1,0:T(8,128)(2,1)S(1)}, u32[]{:S(2)}, u32[]{:S(2)}) collective-permute-start(bf16[4,2,128,128]{3,2,1,0:T(8,128)(2,1)S(1)} %remask.2._.refs_0_.refs_2_), channel_id=1, source_target_pairs={{0,4},{4,8},{8,12},{12,14},{14,10},{10,6},{6,2},{2,0},{1,3},{5,1},... | collective-permute-start | bytes 786440 | tf_op jit(solution)/shard_map/ppermute | solution.py:322
  11.3 6.4 %collective-permute-start.8 = (bf16[4,2,128,128]{3,2,1,0:T(8,128)(2,1)S(1)}, bf16[4,2,128,128]{3,2,1,0:T(8,128)(2,1)S(1)}, u32[]{:S(2)}, u32[]{:S(2)}) collective-permute-start(bf16[4,2,128,128]{3,2,1,0:T(8,128)(2,1)S(1)} %join.6.refs_1_.refs_3_), channel_id=1, source_target_pairs={{0,4},{4,8},{8,12},{12,14},{14,10},{10,6},{6,2},{2,0},{1,3},{5,1},... | collective-permute-start | bytes 786440 | tf_op jit(solution)/shard_map/ppermute | solution.py:322
  13.0 6.5 %collective-permute-start.7 = (bf16[2,4,2,128,128]{4,3,2,1,0:T(8,128)(2,1)S(1)}, bf16[2,4,2,128,128]{4,3,2,1,0:T(8,128)(2,1)S(1)}, u32[]{:S(2)}, u32[]{:S(2)}) collective-permute-start(bf16[2,4,2,128,128]{4,3,2,1,0:T(8,128)(2,1)S(1)} %get-tuple-element.44), channel_id=1, source_target_pairs={{0,1},{1,0},{2,3},{3,2},{4,5},{5,4},{6,7},{7,6},{8,9},{9,8},{10,11... | collective-permute-start | bytes 1572872 | tf_op jit(solution)/shard_map/ppermute | solution.py:322
  14.4 6.4 %collective-permute-start.6 = (bf16[4,2,128,128]{3,2,1,0:T(8,128)(2,1)S(1)}, bf16[4,2,128,128]{3,2,1,0:T(8,128)(2,1)S(1)}, u32[]{:S(2)}, u32[]{:S(2)}) collective-permute-start(bf16[4,2,128,128]{3,2,1,0:T(8,128)(2,1)S(1)} %join.7.refs_0_), channel_id=1, source_target_pairs={{0,4},{4,8},{8,12},{12,14},{14,10},{10,6},{6,2},{2,0},{1,3},{5,1},... | collective-permute-start | bytes 786440 | tf_op jit(solution)/shard_map/ppermute | solution.py:322
  17.7 6.4 %collective-permute-start.11 = (bf16[4,2,128,128]{3,2,1,0:T(8,128)(2,1)S(1)}, bf16[4,2,128,128]{3,2,1,0:T(8,128)(2,1)S(1)}, u32[]{:S(2)}, u32[]{:S(2)}) collective-permute-start(bf16[4,2,128,128]{3,2,1,0:T(8,128)(2,1)S(1)} %join.8.refs_1_), channel_id=1, source_target_pairs={{0,4},{4,8},{8,12},{12,14},{14,10},{10,6},{6,2},{2,0},{1,3},{5,1},... | collective-permute-start | bytes 786440 | tf_op jit(solution)/shard_map/ppermute | solution.py:322
  19.3 4.9 %collective-permute-start.10 = (bf16[2,4,2,128,128]{4,3,2,1,0:T(8,128)(2,1)S(1)}, bf16[2,4,2,128,128]{4,3,2,1,0:T(8,128)(2,1)S(1)}, u32[]{:S(2)}, u32[]{:S(2)}) collective-permute-start(bf16[2,4,2,128,128]{4,3,2,1,0:T(8,128)(2,1)S(1)} %get-tuple-element.49), channel_id=1, source_target_pairs={{0,1},{1,0},{2,3},{3,2},{4,5},{5,4},{6,7},{7,6},{8,9},{9,8},{10,11... | collective-permute-start | bytes 1572872 | tf_op jit(solution)/shard_map/ppermute | solution.py:322
  20.8 6.4 %collective-permute-start.9 = (bf16[4,2,128,128]{3,2,1,0:T(8,128)(2,1)S(1)}, bf16[4,2,128,128]{3,2,1,0:T(8,128)(2,1)S(1)}, u32[]{:S(2)}, u32[]{:S(2)}) collective-permute-start(bf16[4,2,128,128]{3,2,1,0:T(8,128)(2,1)S(1)} %join.9.refs_2_.refs_0_), channel_id=1, source_target_pairs={{0,4},{4,8},{8,12},{12,14},{14,10},{10,6},{6,2},{2,0},{1,3},{5,1},... | collective-permute-start | bytes 786440 | tf_op jit(solution)/shard_map/ppermute | solution.py:322
  24.1 3.0 %collective-permute-start.13 = (bf16[2,4,2,128,128]{4,3,2,1,0:T(8,128)(2,1)S(1)}, bf16[2,4,2,128,128]{4,3,2,1,0:T(8,128)(2,1)S(1)}, u32[]{:S(2)}, u32[]{:S(2)}) collective-permute-start(bf16[2,4,2,128,128]{4,3,2,1,0:T(8,128)(2,1)S(1)} %get-tuple-element.55), channel_id=1, source_target_pairs={{0,1},{1,0},{2,3},{3,2},{4,5},{5,4},{6,7},{7,6},{8,9},{9,8},{10,11... | collective-permute-start | bytes 1572872 | tf_op jit(solution)/shard_map/ppermute | solution.py:322
  27.1 1.5 %collective-permute-start.12 = (bf16[4,2,128,128]{3,2,1,0:T(8,128)(2,1)S(1)}, bf16[4,2,128,128]{3,2,1,0:T(8,128)(2,1)S(1)}, u32[]{:S(2)}, u32[]{:S(2)}) collective-permute-start(bf16[4,2,128,128]{3,2,1,0:T(8,128)(2,1)S(1)} %join.11.refs_2_), channel_id=1, source_target_pairs={{0,1},{1,0},{2,3},{3,2},{4,5},{5,4},{6,7},{7,6},{8,9},{9,8},{10,11... | collective-permute-start | bytes 786440 | tf_op jit(solution)/shard_map/ppermute | solution.py:322
